TPU v7x, 256 devices: a whole 4x4x8 slice. The times are simulated.
256 devices in a mesh: group: 2 (over x_lo), row: 8 (over z), col: 16 (over x_hi, y, core).
Axes of the slice: x: 4 (x_hi: 2, x_lo: 2; x = x_hi * 2 + x_lo), y: 4, z: 8, core: 2. Of those that a mesh axis runs over, the one named last changes fastest.
Arguments:
- pair: bfloat16 [512, 512, 128], P(('group', 'row'), 'col'), may hold values from -6 to 6
- pair_mask: int32 [512, 512], P(('group', 'row'), 'col'), may hold values from 0 to 1, as said below
- tri_proj: bfloat16 [2, 128, 512], replicated, may hold values from -0.5 to 0.5
- tri_gate: bfloat16 [2, 128, 128], replicated, may hold values from -0.5 to 0.5
- triangle_output_weight: bfloat16 [2, 128, 128], replicated, may hold values from -0.5 to 0.5
- tri_gains: float32 [2, 2, 128], replicated, may hold values from 0.1 to 1.9
- pair_bias_gain: float32 [128], replicated, may hold values from 0.1 to 1.9
- bias_weight: bfloat16 [128, 16], replicated, as said below
- tokens: bfloat16 [64, 512, 768], P(('group', 'row')), may hold values from -6 to 6
- att_gain: float32 [768], replicated, may hold values from 0.3 to 3
- att_proj: bfloat16 [4, 768, 768], P(None, None, 'col'), may hold values from -0.21875 to 0.21875
- att_out: bfloat16 [768, 768], replicated, may hold values from -0.21875 to 0.21875
- tr_gain: float32 [768], replicated, may hold values from 0.1 to 1.9
- tr_up: bfloat16 [768, 3072], replicated, may hold values from -0.21875 to 0.21875
- tr_down: bfloat16 [1536, 768], replicated, may hold values from -0.15625 to 0.15625
Outputs:
- pair_out: float32 [512, 512, 128], P(('group', 'row'), 'col')
- tokens_out: float32 [64, 512, 768], P(('group', 'row'), 'col')
Inputs may be any that keep to these rules, and one draw needn't show every extreme that they name: `bias_weight`: a projection of order one to some tens. `pair_mask`: tokens form chains of consecutive tokens; pairs within a chain are mostly valid, pairs across chains rarely.
All inputs are finite; a program needn't handle non-finite values.
Results may differ from a plain program's by a relative error of at most 0.035.
The roundings to bfloat16 on the way count: a program that leaves them out, or rounds other values in their place, can miss the bound.
Values may be sent and summed in bfloat16 or wider, within the bound.
A program may use at most 128 MiB of HBM per device.

v0:
```python
import jax
import jax.numpy as jnp
from jax import lax
from jax.sharding import PartitionSpec as P

EPS = 1e-05


def normalize(value, gain):
    mean = jnp.mean(value, axis=-1, keepdims=True)
    mean_removed = value - mean
    variance = jnp.mean(mean_removed * mean_removed, axis=-1, keepdims=True)
    return mean_removed * lax.rsqrt(variance + EPS) * gain


def edges(state, mask, proj_weight, gate_weight, gain_in):
    normed = normalize(state.astype(jnp.float32), gain_in).astype(jnp.bfloat16)
    proj = jnp.dot(normed, proj_weight, preferred_element_type=jnp.float32)
    width = proj.shape[-1] // 4
    keep = mask.astype(jnp.float32)[..., None]
    left = (keep * jax.nn.sigmoid(proj[..., :width]) * proj[..., width : 2 * width]).astype(
        jnp.bfloat16
    )
    right = (
        keep * jax.nn.sigmoid(proj[..., 2 * width : 3 * width]) * proj[..., 3 * width :]
    ).astype(jnp.bfloat16)
    gate = jax.nn.sigmoid(jnp.dot(normed, gate_weight, preferred_element_type=jnp.float32))
    return (left, right, gate)


def finish(state, summed, gate, out_weight, gain_mid):
    normed = normalize(summed, gain_mid).astype(jnp.bfloat16)
    update = jnp.dot(normed, out_weight, preferred_element_type=jnp.float32)
    return state.astype(jnp.float32) + gate * update


def on_device(
    pair,
    pair_mask,
    tri_proj,
    tri_gate,
    triangle_output_weight,
    tri_gains,
    pair_bias_gain,
    bias_weight,
    tokens,
    att_gain,
    att_proj,
    att_out,
    tr_gain,
    tr_up,
    tr_down,
):
    left, right, gate = edges(pair, pair_mask, tri_proj[0], tri_gate[0], tri_gains[0, 0])
    right_all = lax.all_gather(right, ("group", "row"), axis=0, tiled=True)
    token_block = right_all
    summed = jnp.transpose(
        lax.psum_scatter(
            jnp.einsum("jkc,ikc->jic", token_block, left, preferred_element_type=jnp.float32),
            "col",
            scatter_dimension=0,
            tiled=True,
        ),
        (1, 0, 2),
    )
    state = finish(pair, summed, gate, triangle_output_weight[0], tri_gains[0, 1])
    left, right, gate = edges(state, pair_mask, tri_proj[1], tri_gate[1], tri_gains[1, 0])
    left_all = lax.all_gather(left, "col", axis=1, tiled=True)
    token_block = left_all
    summed = lax.psum_scatter(
        jnp.einsum("kic,kjc->ijc", token_block, right, preferred_element_type=jnp.float32),
        ("group", "row"),
        scatter_dimension=0,
        tiled=True,
    )
    pair_out = finish(state, summed, gate, triangle_output_weight[1], tri_gains[1, 1])
    normed = normalize(pair_out, pair_bias_gain).astype(jnp.bfloat16)
    tile_bias = jnp.dot(normed, bias_weight, preferred_element_type=jnp.float32).astype(
        jnp.bfloat16
    )
    tile_bias = jnp.transpose(tile_bias, (2, 0, 1))
    own_heads = lax.all_to_all(tile_bias, "col", split_axis=0, concat_axis=2, tiled=True)
    head_bias = lax.all_gather(own_heads, ("group", "row"), axis=1, tiled=True)
    noised_samples, length, width = tokens.shape
    local_width = att_proj.shape[2]
    local_heads = head_bias.shape[0]
    head_size = local_width // local_heads
    xn = normalize(tokens.astype(jnp.float32), att_gain).astype(jnp.bfloat16)
    projected = jnp.einsum("snd,fde->fsne", xn, att_proj, preferred_element_type=jnp.float32)
    query = (
        projected[0].astype(jnp.bfloat16).reshape(noised_samples, length, local_heads, head_size)
    )
    keyed = (
        projected[1].astype(jnp.bfloat16).reshape(noised_samples, length, local_heads, head_size)
    )
    value = (
        projected[2].astype(jnp.bfloat16).reshape(noised_samples, length, local_heads, head_size)
    )
    scores = jnp.einsum("sqhe,skhe->shqk", query, keyed, preferred_element_type=jnp.float32)
    scores = scores / jnp.sqrt(jnp.float32(head_size)) + head_bias.astype(jnp.float32)[None]
    weights = jax.nn.softmax(scores, axis=-1).astype(jnp.bfloat16)
    attended = jnp.einsum("shqk,skhe->sqhe", weights, value, preferred_element_type=jnp.float32)
    attended = (
        attended.reshape(noised_samples, length, local_width) * jax.nn.sigmoid(projected[3])
    ).astype(jnp.bfloat16)
    share = length // lax.axis_size("col")
    offset = lax.axis_index("col") * share
    own_tokens = lax.dynamic_slice_in_dim(tokens, offset, share, 1)
    rows_per_head = lax.dynamic_slice_in_dim(
        att_out, lax.axis_index("col") * local_width, local_width, 0
    )
    token_block = attended
    mixed = jnp.transpose(
        lax.psum_scatter(
            jnp.einsum(
                "qmt,tp->mqp", token_block, rows_per_head, preferred_element_type=jnp.float32
            ),
            "col",
            scatter_dimension=0,
            tiled=True,
        ),
        (1, 0, 2),
    )
    first = own_tokens.astype(jnp.float32) + mixed
    xn2 = normalize(first, tr_gain).astype(jnp.bfloat16)
    upped = jnp.dot(xn2, tr_up, preferred_element_type=jnp.float32)
    hidden_width = tr_down.shape[0]
    hidden = (jax.nn.silu(upped[..., :hidden_width]) * upped[..., hidden_width:]).astype(
        jnp.bfloat16
    )
    tokens_out = first + jnp.dot(hidden, tr_down, preferred_element_type=jnp.float32)
    return (pair_out, tokens_out)


def solution(mesh):
    placed = (
        P(("group", "row"), "col", None),
        P(("group", "row"), "col"),
        P(),
        P(),
        P(),
        P(),
        P(),
        P(),
        P(("group", "row"), None, None),
        P(),
        P(None, None, "col"),
        P(),
        P(),
        P(),
        P(),
    )
    return jax.shard_map(
        on_device,
        mesh=mesh,
        in_specs=placed,
        out_specs=(P(("group", "row"), "col", None), P(("group", "row"), "col", None)),
        check_vma=False,
    )
```

profile of v0, /device:TPU:27, one launch (start us, length us, event | category | flops | bytes accessed | tf_op | source)
XLA Modules:
  0.0 690.6 jit_solution(14591083964467103938)
XLA Ops:
  9.3 1.3 fusion.38
  11.4 1.5 fusion.83
  14.0 2.4 copy.95
  16.4 67.5 %all-gather.3.cloned.1.call-done = bf16[512,32,128]{2,1,0:T(8,128)(2,1)} async-done(((bf16[32,32,128]{2,1,0:T(8,128)(2,1)}), bf16[512,32,128]{2,1,0:T(8,128)(2,1)}) %all-gather.3.cloned.1.call-update) | async-done | bytes 4194320 | tf_op jit(solution)/shard_map/all_gather | solution.py:55
  83.9 23.0 %copy.96 = bf16[512,32,128]{1,0,2:T(8,128)(2,1)} copy(bf16[512,32,128]{2,1,0:T(8,128)(2,1)} %all-gather.3.cloned.1.call-done) | data formatting | bytes 8388608 | tf_op jit(solution)/shard_map/all_gather | solution.py:55
  106.9 14.6 %convolution_bitcast_fusion.1 = f32[512,32,128]{0,1,2:T(8,128)} fusion(bf16[32,32,128]{1,0,2:T(8,128)(2,1)S(1)} %copy.95, bf16[512,32,128]{1,0,2:T(8,128)(2,1)} %copy.96), kind=kOutput, calls=%fused_computation.14 | convolution fusion | flops 134217728 | bytes 12845056 | tf_op jit(solution)/shard_map/jkc,ikc->jic/dot_general | solution.py:59
  121.5 11.0 %copy.97 = f32[512,32,128]{2,1,0:T(8,128)} copy(f32[512,32,128]{0,1,2:T(8,128)} %convolution_bitcast_fusion.1) | data formatting | bytes 16777216 | tf_op jit(solution)/shard_map/jkc,ikc->jic/transpose | solution.py:59
  133.5 1.3 fusion.25
  134.7 111.9 %reduce-scatter.3.cloned.1.call-done = f32[32,32,128]{2,1,0:T(8,128)} async-done(((f32[512,32,128]{2,1,0:T(8,128)}), f32[32,32,128]{2,1,0:T(8,128)}) %reduce-scatter.3.cloned.1.call-update) | async-done | bytes 524304 | tf_op jit(solution)/shard_map/reduce_scatter | solution.py:58
  248.0 1.4 multiply_reduce_fusion.3
  249.6 1.4 multiply_convert_fusion.3
  251.0 1.4 fusion.107
  254.6 2.7 copy.103
  257.2 58.8 %all-gather.5.cloned.1.call-done = bf16[32,512,128]{2,1,0:T(8,128)(2,1)} async-done(((bf16[32,32,128]{2,1,0:T(8,128)(2,1)}), bf16[32,512,128]{2,1,0:T(8,128)(2,1)}) %all-gather.5.cloned.1.call-update) | async-done | bytes 4194320 | tf_op jit(solution)/shard_map/all_gather | solution.py:68
  316.0 7.9 %copy.104 = bf16[32,512,128]{1,0,2:T(8,128)(2,1)} copy(bf16[32,512,128]{2,1,0:T(8,128)(2,1)} %all-gather.5.cloned.1.call-done) | data formatting | bytes 8388608 | tf_op jit(solution)/shard_map/all_gather | solution.py:68
  323.9 7.0 %convolution_bitcast_fusion = f32[512,32,128]{0,1,2:T(8,128)} fusion(bf16[32,32,128]{0,1,2:T(8,128)(2,1)} %copy.103, bf16[32,512,128]{1,0,2:T(8,128)(2,1)} %copy.104), kind=kOutput, calls=%fused_computation.13 | convolution fusion | flops 134217728 | bytes 12845056 | tf_op jit(solution)/shard_map/kic,kjc->ijc/dot_general | solution.py:71
  330.9 10.9 %copy.105 = f32[512,32,128]{2,1,0:T(8,128)} copy(f32[512,32,128]{0,1,2:T(8,128)} %convolution_bitcast_fusion) | data formatting | bytes 16777216 | tf_op jit(solution)/shard_map/kic,kjc->ijc/transpose | solution.py:71
  341.9 2.5 convert_reduce_fusion
  345.8 1.3 fusion.22
  347.1 95.4 %reduce-scatter.5.cloned.1.call-done = f32[32,32,128]{2,1,0:T(8,128)} async-done(((f32[512,32,128]{2,1,0:T(8,128)}), f32[32,32,128]{2,1,0:T(8,128)}) %reduce-scatter.5.cloned.1.call-update) | async-done | bytes 524304 | tf_op jit(solution)/shard_map/reduce_scatter | solution.py:70
  443.8 1.4 multiply_reduce_fusion.1
  445.2 1.8 fusion.108
  448.8 6.8 all-to-all-start
  455.6 4.8 fusion.109
  461.6 27.3 %all_gather.11 = bf16[1,512,512]{2,1,0:T(8,128)(2,1)S(1)} all-gather(bf16[1,32,512]{2,1,0:T(8,128)(2,1)S(1)} %all_to_all.16), channel_id=1, replica_groups=mesh['group'=2,'row'=8,'col'=16] {'group','row'}, dimensions={1}, use_global_device_ids=true | all-gather | bytes 557056 | tf_op jit(solution)/shard_map/all_gather | solution.py:83
  489.1 1.3 copy.112
  490.4 5.0 fusion.110
  495.4 6.4 convolution_bitcast_fusion.2
  501.8 7.8 %copy.114 = f32[512,4,768]{2,1,0:T(4,128)} copy(f32[512,4,768]{0,2,1:T(8,128)} %convolution_bitcast_fusion.2) | data formatting | bytes 12582912 | tf_op jit(solution)/shard_map/qmt,tp->mqp/transpose | solution.py:115
  511.5 163.7 %all-reduce.3.cloned.1.call-done = f32[512,4,768]{2,1,0:T(4,128)} async-done(((f32[512,4,768]{2,1,0:T(4,128)}), f32[512,4,768]{2,1,0:T(4,128)}) %all-reduce.3.cloned.1.call-update) | async-done | bytes 6291472
  678.5 3.3 fusion.6
  681.8 2.3 fusion.28
  (75 shorter events, 18.8 us)
Async XLA Ops:
  7.2 674.7 %copy-start = (bf16[1536,768]{1,0:T(8,128)(2,1)S(1)}, bf16[1536,768]{1,0:T(8,128)(2,1)}, u32[]{:S(2)}) copy-start(bf16[1536,768]{1,0:T(8,128)(2,1)} %param.29) | copy-start | bytes 7077892
  7.2 76.7 %all-gather.3.cloned.1.call-start = ((), (), s32[]{:S(2)}) async-start(), calls=%async_computation.3 | async-start | bytes 4456448 | tf_op jit(solution)/shard_map/all_gather | solution.py:55
  13.9 232.6 %reduce-scatter.3.cloned.1.call-start = ((), (), s32[]{:S(2)}) async-start(), calls=%async_computation.4 | async-start | bytes 8912896 | tf_op jit(solution)/shard_map/reduce_scatter | solution.py:58
  132.5 0.9 copy-start.3
  132.5 1.0 copy-start.9
  132.5 118.4 %copy-start.6 = (bf16[2,128,128]{2,1,0:T(8,128)(2,1)S(1)}, bf16[2,128,128]{2,1,0:T(8,128)(2,1)}, u32[]{:S(2)}) copy-start(bf16[2,128,128]{2,1,0:T(8,128)(2,1)} %param.19) | copy-start | bytes 196612
  132.6 120.3 %copy-start.4 = (bf16[2,128,512]{2,1,0:T(8,128)(2,1)S(1)}, bf16[2,128,512]{2,1,0:T(8,128)(2,1)}, u32[]{:S(2)}) copy-start(bf16[2,128,512]{2,1,0:T(8,128)(2,1)} %param.17) | copy-start | bytes 786436
  132.6 183.5 %all-gather.5.cloned.1.call-start = ((), (), s32[]{:S(2)}) async-start(), calls=%async_computation.5 | async-start | bytes 4456448 | tf_op jit(solution)/shard_map/all_gather | solution.py:68
  254.4 188.1 %reduce-scatter.5.cloned.1.call-start = ((), (), s32[]{:S(2)}) async-start(), calls=%async_computation.6 | async-start | bytes 8912896 | tf_op jit(solution)/shard_map/reduce_scatter | solution.py:70
  341.8 2.8 copy-start.1
  341.9 3.9 copy-start.10
  344.7 102.7 %copy-start.7 = (bf16[128,16]{0,1:T(8,128)(2,1)S(1)}, bf16[128,16]{0,1:T(8,128)(2,1)}, u32[]{:S(2)}) copy-start(bf16[128,16]{0,1:T(8,128)(2,1)} %param.22) | copy-start | bytes 12292
  344.7 102.7 %copy-start.8 = (f32[128]{0:T(128)S(1)}, f32[128]{0:T(128)}, u32[]{:S(2)}) copy-start(f32[128]{0:T(128)} %param.21) | copy-start | bytes 1540
  447.0 13.5 %copy-start.2 = (f32[32,32,128]{2,1,0:T(8,128)}, f32[32,32,128]{2,1,0:T(8,128)S(1)}, u32[]{:S(2)}) copy-start(f32[32,32,128]{2,1,0:T(8,128)S(1)} %get-tuple-element.15) | copy-start | bytes 1572868
  448.8 12.5 %all-to-all-start = ((bf16[16,2,512]{2,1,0:T(2,128)(2,1)}), bf16[16,2,512]{2,1,0:T(2,128)(2,1)S(1)}, u32[]{:S(2)}, u32[]{:S(2)}) async-start(bf16[16,2,512]{2,1,0:T(2,128)(2,1)} %reshape.155), calls=%async_computation.2 | async-start | bytes 65536 | tf_op jit(solution)/shard_map/all_to_all | solution.py:82
  455.6 219.6 %all-reduce.3.cloned.1.call-start = ((), (), s32[]{:S(2)}) async-start(), calls=%async_computation.7 | async-start | bytes 12582912
  509.6 0.7 copy-start.11
  509.6 168.9 %copy-start.5 = (f32[768]{0:T(1024)S(1)}, f32[768]{0:T(1024)}, u32[]{:S(2)}) copy-start(f32[768]{0:T(1024)} %param.27) | copy-start | bytes 9220
Sparse Core Ops, SparseCore 0:
  14.1 69.7 all-gather.2
  132.7 113.8 reduce-scatter.2
  254.5 61.4 all-gather.4
  342.0 100.4 reduce-scatter.4
  509.7 165.4 all-reduce.2
where the time goes:
time: 692 us; the launch traced here: 691 us
  waiting for transfers between devices  498 us (72%)
  local copies, waits for them, and re-layouts  72.7 us (11%)
  matrix products  51.5 us (7%)
  blocking collectives  27.3 us (4%)
  other arithmetic  18.8 us (3%)
  between operations  14.8 us (2%)
  starting transfers between devices  7.23 us (1%)
    unnamed x6, waiting for transfers between devices  164 us
    reduce_scatter x1, waiting for transfers between devices, on_device(): lax.psum_scatter(jnp.einsum('jkc,ikc->jic', token_block, left, preferred_...  112 us
    reduce_scatter x1, waiting for transfers between devices, on_device(): lax.psum_scatter(jnp.einsum('kic,kjc->ijc', token_block, right, preferred...  95.4 us
    all_gather x1, waiting for transfers between devices, on_device(): right_all = lax.all_gather(right, ('group', 'row'), axis=0, tiled=True)  67.5 us
    all_gather x1, waiting for transfers between devices, on_device(): left_all = lax.all_gather(left, 'col', axis=1, tiled=True)  58.8 us
    all_gather x1, blocking collectives, on_device(): head_bias = lax.all_gather(own_heads, ('group', 'row'), axis=1, tiled=True)  27.3 us
    all_gather x1, local copies, waits for them, and re-layouts, on_device(): right_all = lax.all_gather(right, ('group', 'row'), axis=0, tiled=True)  23 us
    dot_general x1, matrix products, on_device(): jnp.einsum('jkc,ikc->jic', token_block, left, preferred_element_type=jnp....  14.6 us
  transfers between devices with their start and end apart: 6, of which 6 were waited for; matrix products, arithmetic and copies ran while one was open for 2% of the time, Pallas kernels for 0%

commit v1 on v0

v1 whole, which is shorter than its diff:
```python
import jax
import jax.numpy as jnp
from jax import lax
from jax.experimental import pallas as pl
from jax.experimental.pallas import tpu as pltpu
from jax.sharding import PartitionSpec as P

EPS = 1e-05
MESH = pl.DeviceIdType.MESH
F32 = jnp.float32
BF16 = jnp.bfloat16
NT = (((1,), (1,)), ((), ()))
TN = (((0,), (0,)), ((), ()))


def normalize(value, gain):
    mean = jnp.mean(value, axis=-1, keepdims=True)
    mean_removed = value - mean
    variance = jnp.mean(mean_removed * mean_removed, axis=-1, keepdims=True)
    return mean_removed * lax.rsqrt(variance + EPS) * gain


def mm(a, b, dims=(((1,), (0,)), ((), ()))):
    return lax.dot_general(a, b, dims, preferred_element_type=F32)


def swap_map(lane, inner):
    a, b, k = lane >> 7, (lane >> 5) & 3, lane & 31
    if inner:
        k = ((k & 3) << 3) + (k >> 2)
    return (b << 7) + (a << 5) + k


def swap_matrix(inner, transposed=False):
    row = lax.broadcasted_iota(jnp.int32, (512, 512), 0)
    col = lax.broadcasted_iota(jnp.int32, (512, 512), 1)
    if transposed:
        hit = row == swap_map(col, inner)
    else:
        hit = swap_map(row, inner) == col
    return jnp.where(hit, 1.0, 0.0).astype(BF16)


def remote(src, dst, send, recv, device):
    return pltpu.make_async_remote_copy(
        src_ref=src,
        dst_ref=dst,
        send_sem=send,
        recv_sem=recv,
        device_id=device,
        device_id_type=MESH,
    )


class Exchange:
    def __init__(self, n, me, device, src, dst, send, recv):
        self.n, self.me, self.device = n, me, device
        self.src, self.dst, self.send, self.recv = src, dst, send, recv

    def copy(self, d):
        peer = lax.rem(self.me + d, self.n)
        return remote(
            self.src(peer), self.dst(self.me), self.send.at[d], self.recv.at[d], self.device(peer)
        )

    def own(self):
        return pltpu.make_async_copy(self.src(self.me), self.dst(self.me), self.recv.at[0])

    def start(self):
        def body(d, carry):
            self.copy(d).start()
            return carry

        lax.fori_loop(1, self.n, body, 0)
        self.own().start()

    def wait(self):
        self.own().wait()

        def body(d, carry):
            self.copy(d).wait()
            return carry

        lax.fori_loop(1, self.n, body, 0)


def pair_kernel(
    pair_ref,
    mask_ref,
    wp_ref,
    wg_ref,
    wo_ref,
    gin_ref,
    gmid_ref,
    bgain_ref,
    bw_ref,
    out_ref,
    bias_ref,
    z_s,
    gate_s,
    flat_s,
    nrm_s,
    send_a,
    recv_a,
    send_b,
    recv_b,
    x_left,
    x_right,
    send_bt,
    recv_bt,
    send_at,
    recv_at,
    heads_s,
    recv_h,
    rows_s,
    ssem,
    rsem,
):
    group, row, col = (lax.axis_index(name) for name in ("group", "row", "col"))
    big = group * 8 + row
    quad = col // 2
    core = lax.rem(col, 2)

    def on_col(peer):
        return {"col": peer}

    def on_quad(peer):
        return {"col": peer * 2 + core}

    def on_rows(peer):
        return {"group": peer // 8, "row": lax.rem(peer, 8)}

    barrier = pltpu.get_barrier_semaphore()

    def greet_col(d, carry):
        pl.semaphore_signal(
            barrier, inc=1, device_id=on_col(lax.rem(col + d, 16)), device_id_type=MESH
        )
        return carry

    def greet_rows(d, carry):
        pl.semaphore_signal(
            barrier, inc=1, device_id=on_rows(lax.rem(big + d, 16)), device_id_type=MESH
        )
        return carry

    lax.fori_loop(1, 16, greet_col, 0)
    lax.fori_loop(1, 16, greet_rows, 0)

    swap_in = swap_matrix(True)
    swap_out = swap_matrix(True, transposed=True)

    def edges(m, state):
        for it in range(8):
            zn = normalize(state(it), gin_ref[m]).astype(BF16)
            gate_s[pl.ds(it * 128, 128), :] = jax.nn.sigmoid(mm(zn, wg_ref[m]))
            proj = mm(wp_ref[m], zn, NT)
            keep = mask_ref[it : it + 1, :]
            left = keep * jax.nn.sigmoid(proj[0:128]) * proj[128:256]
            right = keep * jax.nn.sigmoid(proj[256:384]) * proj[384:512]
            flat_s[pl.ds(it, 128, stride=16), :] = left
            flat_s[pl.ds(8 + it, 128, stride=16), :] = right
        for s in range(8):
            send_a[m, s] = flat_s[pl.ds(s * 256, 256), :].astype(BF16)

    def triangle(m):
        go_a = Exchange(
            8,
            quad,
            on_quad,
            lambda p: send_a.at[m, p],
            lambda p: recv_a.at[m, p],
            ssem.at[5 * m],
            rsem.at[5 * m],
        )
        go_a.start()
        go_a.wait()
        for hi in range(2):
            lanes = jnp.concatenate([recv_a[m, hi * 4 + lo] for lo in range(4)], axis=1)
            moved = mm(lanes, swap_in)
            parts = [moved[:, lo * 128 : (lo + 1) * 128].reshape(32, 8, 128) for lo in range(4)]
            send_b[m, :, :, hi * 128 : (hi + 1) * 128] = jnp.concatenate(parts, axis=1).astype(BF16)
        go_b = Exchange(
            16,
            big,
            on_rows,
            lambda p: send_b.at[m, pl.ds(p * 2, 2)],
            lambda p: recv_b.at[m, p // 2, lax.rem(p, 2)],
            ssem.at[5 * m + 1],
            rsem.at[5 * m + 1],
        )
        go_b.start()
        go_b.wait()
        partner = on_col(quad * 2 + 1 - core)
        cross = remote(
            recv_b.at[m, :, :, 0],
            x_left.at[m],
            ssem.at[5 * m + 2, 0],
            rsem.at[5 * m + 2, 0],
            partner,
        )
        cross.start()
        if m == 0:
            cross_right = remote(
                recv_b.at[m, :, 1 - core, 1],
                x_right,
                ssem.at[5 * m + 2, 1],
                rsem.at[5 * m + 2, 1],
                partner,
            )
            cross_right.start()
            left = recv_b[m, :, :, 0].reshape(512, 256)
            right = recv_b[m, :, core, 1].reshape(256, 256)
            total = mm(left, right, NT)
            cross.wait()
            cross_right.wait()
            total += mm(x_left[m].reshape(512, 256), x_right[...].reshape(256, 256), NT)
            send_bt[m] = total.reshape(8, 2, 32, 256).astype(BF16)
        else:
            right = recv_b[m, :, :, 1].reshape(512, 256)
            own = mm(recv_b[m, :, :, 0].reshape(512, 256), right, TN)
            send_bt[m, :, core] = own.reshape(8, 32, 256).astype(BF16)
            cross.wait()
            other = mm(x_left[m].reshape(512, 256), right, TN)
            send_bt[m, :, 1 - core] = other.reshape(8, 32, 256).astype(BF16)
        back_b = Exchange(
            16,
            big,
            on_rows,
            lambda p: send_bt.at[m, p // 2, lax.rem(p, 2)],
            lambda p: recv_bt.at[m, p],
            ssem.at[5 * m + 3],
            rsem.at[5 * m + 3],
        )
        back_b.start()
        back_b.wait()
        for hi in range(2):
            block = recv_bt[m, :, :, hi * 128 : (hi + 1) * 128].astype(F32)
            lanes = jnp.concatenate(
                [block[:, lo * 8 : (lo + 1) * 8, :].reshape(128, 128) for lo in range(4)], axis=1
            ).astype(BF16)
            moved = mm(lanes, swap_out).astype(BF16)
            for lo in range(4):
                send_at[m, hi * 4 + lo] = moved[:, lo * 128 : (lo + 1) * 128]
        back_a = Exchange(
            8,
            quad,
            on_quad,
            lambda p: send_at.at[m, p],
            lambda p: recv_at.at[m, p],
            ssem.at[5 * m + 4],
            rsem.at[5 * m + 4],
        )
        back_a.start()
        back_a.wait()
        summed = recv_at[m].astype(F32).reshape(128, 8, 128)
        mean = jnp.sum(summed, axis=0, keepdims=True) * (1.0 / 128)
        mean_removed = summed - mean
        variance = jnp.sum(mean_removed * mean_removed, axis=0, keepdims=True) * (1.0 / 128)
        nrm_s[...] = (mean_removed * lax.rsqrt(variance + EPS)).reshape(1024, 128)

    def update(m, it):
        normed = (nrm_s[pl.ds(it, 128, stride=8), :] * gmid_ref[m]).astype(BF16)
        return gate_s[pl.ds(it * 128, 128), :] * mm(normed, wo_ref[m], TN)

    def first_state(it):
        return pair_ref[pl.ds(it * 128, 128), :].astype(F32)

    def second_state(it):
        z = first_state(it) + update(0, it)
        z_s[pl.ds(it * 128, 128), :] = z
        return z

    edges(0, first_state)
    pl.semaphore_wait(barrier, 30)
    triangle(0)
    edges(1, second_state)
    triangle(1)
    for it in range(8):
        z = z_s[pl.ds(it * 128, 128), :] + update(1, it)
        out_ref[pl.ds(it * 128, 128), :] = z
        zn = normalize(z, bgain_ref[...]).astype(BF16)
        bias = mm(bw_ref[...], zn, NT).astype(BF16).astype(F32)
        heads_s[pl.ds(it, 16, stride=8), :] = bias
    to_head = Exchange(
        16,
        col,
        on_col,
        lambda p: heads_s.at[pl.ds(p * 8, 8)],
        lambda p: recv_h.at[p],
        ssem.at[10],
        rsem.at[10],
    )
    to_head.start()
    to_head.wait()
    lanes = jnp.concatenate(
        [
            jnp.concatenate([recv_h[hi * 4 + lo] for lo in range(4)], axis=1)
            for hi in range(4)
        ],
        axis=0,
    ).astype(BF16)
    moved = mm(lanes, swap_matrix(False))
    for hi in range(4):
        for lo in range(4):
            rows_s[pl.ds(hi * 32 + lo, 8, stride=4), :] = moved[
                hi * 8 : (hi + 1) * 8, lo * 128 : (lo + 1) * 128
            ]
    bias_ref[big] = jnp.concatenate(
        [rows_s[hi * 32 : (hi + 1) * 32, :] for hi in range(4)], axis=1
    ).astype(BF16)
    spread = Exchange(
        16,
        big,
        on_rows,
        lambda p: bias_ref.at[big],
        lambda p: bias_ref.at[p],
        ssem.at[11],
        rsem.at[11],
    )

    def spread_start(d, carry):
        spread.copy(d).start()
        return carry

    def spread_wait(d, carry):
        spread.copy(d).wait()
        return carry

    lax.fori_loop(1, 16, spread_start, 0)
    lax.fori_loop(1, 16, spread_wait, 0)


def pair_part(
    pair, pair_mask, tri_proj, tri_gate, triangle_output_weight, tri_gains, pair_bias_gain, bias_weight
):
    vmem = pl.BlockSpec(memory_space=pltpu.VMEM)
    pair_out, head_bias = pl.pallas_call(
        pair_kernel,
        out_shape=(
            jax.ShapeDtypeStruct((1024, 128), F32),
            jax.ShapeDtypeStruct((16, 32, 512), BF16),
        ),
        in_specs=[vmem] * 9,
        out_specs=(vmem, vmem),
        scratch_shapes=[
            pltpu.VMEM((1024, 128), F32),
            pltpu.VMEM((1024, 128), F32),
            pltpu.VMEM((2048, 128), F32),
            pltpu.VMEM((1024, 128), F32),
            pltpu.VMEM((2, 8, 256, 128), BF16),
            pltpu.VMEM((2, 8, 256, 128), BF16),
            pltpu.VMEM((2, 32, 32, 256), BF16),
            pltpu.VMEM((2, 8, 2, 2, 32, 256), BF16),
            pltpu.VMEM((2, 8, 2, 32, 256), BF16),
            pltpu.VMEM((8, 32, 256), BF16),
            pltpu.VMEM((2, 8, 2, 32, 256), BF16),
            pltpu.VMEM((2, 16, 32, 256), BF16),
            pltpu.VMEM((2, 8, 128, 128), BF16),
            pltpu.VMEM((2, 8, 128, 128), BF16),
            pltpu.VMEM((128, 128), F32),
            pltpu.VMEM((16, 8, 128), F32),
            pltpu.VMEM((128, 128), F32),
            pltpu.SemaphoreType.DMA((12, 16)),
            pltpu.SemaphoreType.DMA((12, 16)),
        ],
        compiler_params=pltpu.CompilerParams(
            collective_id=0, has_side_effects=True, vmem_limit_bytes=40 * 1024 * 1024
        ),
        cost_estimate=pl.CostEstimate(
            flops=1_500_000_000, bytes_accessed=3_000_000, transcendentals=1_500_000
        ),
    )(
        pair.reshape(1024, 128),
        pair_mask.reshape(8, 128).astype(F32),
        jnp.swapaxes(tri_proj, 1, 2),
        tri_gate,
        triangle_output_weight,
        tri_gains[:, 0:1, :],
        jnp.broadcast_to(tri_gains[:, 1, :, None], (2, 128, 128)),
        pair_bias_gain.reshape(1, 128),
        jnp.swapaxes(bias_weight, 0, 1),
    )
    return pair_out.reshape(32, 32, 128), head_bias.reshape(512, 512)


def on_device(
    pair,
    pair_mask,
    tri_proj,
    tri_gate,
    triangle_output_weight,
    tri_gains,
    pair_bias_gain,
    bias_weight,
    tokens,
    att_gain,
    att_proj,
    att_out,
    tr_gain,
    tr_up,
    tr_down,
):
    pair_out, head_bias = pair_part(
        pair,
        pair_mask,
        tri_proj,
        tri_gate,
        triangle_output_weight,
        tri_gains,
        pair_bias_gain,
        bias_weight,
    )
    samples, length, width = tokens.shape
    head_size = att_proj.shape[2]
    xn = normalize(tokens.astype(F32), att_gain).astype(BF16)
    projected = jnp.einsum("snd,fde->fsne", xn, att_proj, preferred_element_type=F32)
    query, keyed, value = (projected[i].astype(BF16) for i in range(3))
    scores = jnp.einsum("sqe,ske->sqk", query, keyed, preferred_element_type=F32)
    scores = scores / jnp.sqrt(F32(head_size)) + head_bias.astype(F32)[None]
    weights = jax.nn.softmax(scores, axis=-1).astype(BF16)
    attended = jnp.einsum("sqk,ske->sqe", weights, value, preferred_element_type=F32)
    attended = (attended * jax.nn.sigmoid(projected[3])).astype(BF16)
    attended = lax.all_to_all(attended, "col", split_axis=1, concat_axis=2, tiled=True)
    share = length // lax.axis_size("col")
    own_tokens = lax.dynamic_slice_in_dim(tokens, lax.axis_index("col") * share, share, 1)
    mixed = jnp.dot(attended, att_out, preferred_element_type=F32)
    first = own_tokens.astype(F32) + mixed
    xn2 = normalize(first, tr_gain).astype(BF16)
    upped = jnp.dot(xn2, tr_up, preferred_element_type=F32)
    hidden_width = tr_down.shape[0]
    hidden = (jax.nn.silu(upped[..., :hidden_width]) * upped[..., hidden_width:]).astype(BF16)
    tokens_out = first + jnp.dot(hidden, tr_down, preferred_element_type=F32)
    return (pair_out, tokens_out)


def solution(mesh):
    placed = (
        P(("group", "row"), "col", None),
        P(("group", "row"), "col"),
        P(),
        P(),
        P(),
        P(),
        P(),
        P(),
        P(("group", "row"), None, None),
        P(),
        P(None, None, "col"),
        P(),
        P(),
        P(),
        P(),
    )
    return jax.shard_map(
        on_device,
        mesh=mesh,
        in_specs=placed,
        out_specs=(P(("group", "row"), "col", None), P(("group", "row"), "col", None)),
        check_vma=False,
    )
```

time: 692 us -> 173 us (0.25)
  the two profiles are of different devices: /device:TPU:27 before, /device:TPU:1 now
where the time goes in v1:
time: 173 us; the launch traced here: 172 us
  Pallas kernels  117 us (68%)
  matrix products  17.5 us (10%)
  local copies, waits for them, and re-layouts  16.5 us (10%)
  waiting for transfers between devices  8.29 us (5%)
  other arithmetic  5.83 us (3%)
  starting transfers between devices  5.77 us (3%)
    pallas_call x1, Pallas kernels, pair_part(): pl.pallas_call(pair_kernel, out_shape=(jax.ShapeDtypeStruct((1024, 128),...  117 us
    unnamed x24, local copies, waits for them, and re-layouts  9.08 us
    all_to_all x1, waiting for transfers between devices, on_device(): lax.all_to_all(attended, 'col', split_axis=1, concat_axis=2, tiled=True)  8.29 us
    all_to_all x1, starting transfers between devices, on_device(): lax.all_to_all(attended, 'col', split_axis=1, concat_axis=2, tiled=True)  5.77 us
    sub x1, matrix products, on_device(): weights = jax.nn.softmax(scores, axis=-1).astype(BF16)  4.89 us
    dot_general x1, matrix products, on_device(): jnp.einsum('sqk,ske->sqe', weights, value, preferred_element_type=F32)  3.54 us
  transfers between devices with their start and end apart: 1, of which 1 were waited for; matrix products, arithmetic and copies ran while one was open for 0% of the time, Pallas kernels for 0%

profile of v1, /device:TPU:1, one launch (start us, length us, event | category | flops | bytes accessed | tf_op | source)
XLA Modules:
  0.0 172.1 jit_solution(15488236753936649584)
XLA Ops:
  0.6 0.0 copy-start
  0.6 0.9 convert_element_type.48
  1.5 0.1 convert_element_type.49.mask_ref
  1.6 1.1 copy.25
  2.7 0.8 fusion.42
  3.5 0.1 broadcast_in_dim.5.gmid_ref
  3.6 0.9 copy-done.1
  4.5 0.8 copy-done.2
  5.4 0.8 copy-done.3
  6.2 0.7 copy-done.4
  6.9 0.7 copy-done.5
  7.6 117.3 %shard_map.158 = (f32[1024,128]{1,0:T(8,128)S(1)}, bf16[16,32,512]{2,1,0:T(8,128)(2,1)S(1)}) custom-call(bf16[1024,128]{1,0:T(8,128)(2,1)S(1)} %bitcast.79, f32[8,128]{1,0:T(8,128)S(1)} %convert_element_type.49.mask_ref, bf16[2,512,128]{2,1,0:T(8,128)(2,1)S(1)} %bitcast.78, bf16[2,128,128]{2,1,0:T(8,128)(2,1)S(1)} %copy-done.2, ...), custom_call_target="tpu_custom_call" | custom-call | flops 1500000000 | bytes 3000000 | tf_op jit(solution)/shard_map/pallas_call | solution.py:338
  124.9 1.2 bitcast_convert_fusion
  126.1 2.6 %copy.26 = f32[512,512]{0,1:T(8,128)} copy(f32[512,512]{1,0:T(8,128)} %bitcast_convert_fusion) | data formatting | bytes 2097152 | tf_op jit(solution)/shard_map/convert_element_type | solution.py:420
  128.7 2.5 %convert_reduce_fusion = f32[4,512]{1,0:T(4,128)S(1)} fusion(bf16[4,512,768]{2,1,0:T(8,128)(2,1)} %param.23), kind=kLoop, calls=%fused_computation.2 | loop fusion | flops 3143680 | bytes 3153920 | tf_op jit(solution)/shard_map/reduce_sum | solution.py:17
  131.2 0.3 copy-done.6
  131.5 1.1 fusion.3
  132.6 2.9 %fusion.43 = (bf16[4,4,512,48]{2,3,0,1:T(8,128)(2,1)}, f32[4,4,512,48]{2,3,0,1:T(8,128)}) fusion(bf16[4,768,48]{1,2,0:T(8,128)(2,1)S(1)} %copy-done.8, bf16[4,512,768]{2,1,0:T(8,128)(2,1)S(1)} %copy-done.6, f32[768]{0:T(1024)S(1)} %copy-done.9, f32[4,512]{1,0:T(4,128)S(1)} %add_rsqrt_fusion, f32[4,512]{1,0:T(4,128)S(1)} %broadcast_multiply_fusion), kind=kOutput, calls=%fused_computation.55 | convolution fusion | flops 612237312 | bytes 5819392 | tf_op jit(solution)/shard_map/snd,fde->fsne/dot_general | solution.py:417
  135.5 4.9 %fusion.44 = (f32[4,512]{1,0:T(4,128)S(1)}, f32[4,512,512]{1,2,0:T(8,128)}) fusion(f32[512,512]{0,1:T(8,128)} %copy.26, bf16[4,4,512,48]{2,3,0,1:T(8,128)(2,1)} %get-tuple-element.8), kind=kOutput, calls=%fused_computation.56 | convolution fusion | flops 104858112 | bytes 5644288 | tf_op jit(solution)/shard_map/sub | solution.py:421
  140.4 3.5 %fusion.25 = bf16[4,512,48]{1,2,0:T(8,128)(2,1)} fusion(f32[4,512,512]{1,2,0:T(8,128)} %get-tuple-element.11, f32[4,512]{1,0:T(4,128)S(1)} %get-tuple-element.10, f32[4,4,512,48]{2,3,0,1:T(8,128)} %get-tuple-element.9, bf16[4,4,512,48]{2,3,0,1:T(8,128)(2,1)} %get-tuple-element.8), kind=kOutput, calls=%fused_computation.26 | convolution fusion | flops 103251968 | bytes 4988928 | tf_op jit(solution)/shard_map/sqk,ske->sqe/dot_general | solution.py:422
  143.9 1.3 copy.28
  145.2 1.5 reshape.70
  146.6 5.8 %all-to-all-start = ((bf16[16,2,3072]{2,1,0:T(2,128)(2,1)}), bf16[16,2,3072]{2,1,0:T(2,128)(2,1)}, u32[]{:S(2)}, u32[]{:S(2)}) async-start(bf16[16,2,3072]{2,1,0:T(2,128)(2,1)} %reshape.70), calls=%async_computation | async-start | bytes 393216 | tf_op jit(solution)/shard_map/all_to_all | solution.py:424
  152.4 8.3 %all-to-all-done = bf16[16,2,3072]{2,1,0:T(2,128)(2,1)} async-done(((bf16[16,2,3072]{2,1,0:T(2,128)(2,1)}), bf16[16,2,3072]{2,1,0:T(2,128)(2,1)}, u32[]{:S(2)}, u32[]{:S(2)}) %all-to-all-start) | async-done | bytes 196640 | tf_op jit(solution)/shard_map/all_to_all | solution.py:424
  160.7 1.4 reshape.71
  162.1 1.1 copy.36
  163.3 1.5 all_to_all.16
  164.8 1.7 fusion.45
  166.5 0.2 multiply_reduce_fusion
  166.8 3.2 %fusion.6 = f32[4,32,3072]{2,1,0:T(8,128)S(1)} fusion(bf16[768,3072]{1,0:T(8,128)(2,1)} %param.28, f32[4,32,768]{2,1,0:T(8,128)S(1)} %get-tuple-element.13, f32[768]{0:T(1024)S(1)} %copy-done.7, f32[4,32]{1,0:T(4,128)S(1)} %add_rsqrt_fusion.1, f32[4,32]{1,0:T(4,128)S(1)} %broadcast_multiply_fusion.1), kind=kOutput, calls=%fused_computation.8 | convolution fusion | flops 604372992 | bytes 6688768 | tf_op jit(solution)/shard_map/dot_general | solution.py:430
  169.9 1.4 fusion.20
  171.3 0.8 copy.38
  (17 shorter events, 0.1 us)
Async XLA Ops:
  0.6 169.3 %copy-start = (bf16[1536,768]{1,0:T(8,128)(2,1)S(1)}, bf16[1536,768]{1,0:T(8,128)(2,1)}, u32[]{:S(2)}) copy-start(bf16[1536,768]{1,0:T(8,128)(2,1)} %param.29) | copy-start | bytes 7077892
  3.6 1.0 copy-start.1
  4.5 0.8 copy-start.2
  5.4 0.8 copy-start.3
  6.2 0.7 copy-start.4
  6.9 0.7 copy-start.5
  126.1 6.5 %copy-start.8 = (bf16[4,768,48]{1,2,0:T(8,128)(2,1)S(1)}, bf16[4,768,48]{1,2,0:T(8,128)(2,1)}, u32[]{:S(2)}) copy-start(bf16[4,768,48]{1,2,0:T(8,128)(2,1)} %param.25) | copy-start | bytes 884740
  126.1 6.5 %copy-start.9 = (f32[768]{0:T(1024)S(1)}, f32[768]{0:T(1024)}, u32[]{:S(2)}) copy-start(f32[768]{0:T(1024)} %param.24) | copy-start | bytes 9220
  128.7 2.8 %copy-start.6 = (bf16[4,512,768]{2,1,0:T(8,128)(2,1)S(1)}, bf16[4,512,768]{2,1,0:T(8,128)(2,1)}, u32[]{:S(2)}) copy-start(bf16[4,512,768]{2,1,0:T(8,128)(2,1)} %param.23) | copy-start | bytes 9437188
  143.9 22.8 %copy-start.7 = (f32[768]{0:T(1024)S(1)}, f32[768]{0:T(1024)}, u32[]{:S(2)}) copy-start(f32[768]{0:T(1024)} %param.27) | copy-start | bytes 9220
  146.6 14.1 %all-to-all-start = ((bf16[16,2,3072]{2,1,0:T(2,128)(2,1)}), bf16[16,2,3072]{2,1,0:T(2,128)(2,1)}, u32[]{:S(2)}, u32[]{:S(2)}) async-start(bf16[16,2,3072]{2,1,0:T(2,128)(2,1)} %reshape.70), calls=%async_computation | async-start | bytes 393216 | tf_op jit(solution)/shard_map/all_to_all | solution.py:424

commit v2 on v1

--- a/solution.py
+++ b/solution.py
@@ -84,43 +84,71 @@
         lax.fori_loop(1, self.n, body, 0)
 
 
-def pair_kernel(
-    pair_ref,
-    mask_ref,
-    wp_ref,
-    wg_ref,
-    wo_ref,
-    gin_ref,
-    gmid_ref,
-    bgain_ref,
-    bw_ref,
-    out_ref,
-    bias_ref,
-    z_s,
-    gate_s,
-    flat_s,
-    nrm_s,
-    send_a,
-    recv_a,
-    send_b,
-    recv_b,
-    x_left,
-    x_right,
-    send_bt,
-    recv_bt,
-    send_at,
-    recv_at,
-    heads_s,
-    recv_h,
-    rows_s,
-    ssem,
-    rsem,
-):
+NAMES = (
+    "pair",
+    "mask",
+    "wp",
+    "wg",
+    "wo",
+    "gains",
+    "bgain",
+    "bw",
+    "tokens",
+    "again",
+    "watt",
+    "wout",
+    "tgain",
+    "wup",
+    "wdown",
+)
+
+
+def block_kernel(*refs):
+    inputs = dict(zip(NAMES, refs[:15]))
+    out_ref, tok_ref = refs[15:17]
+    held = dict(zip(NAMES, refs[17:32]))
+    (
+        z_s,
+        gate_s,
+        flat_s,
+        nrm_s,
+        send_a,
+        recv_a,
+        send_b,
+        recv_b,
+        x_left,
+        x_right,
+        send_bt,
+        recv_bt,
+        send_at,
+        recv_at,
+        heads_s,
+        recv_h,
+        rows_s,
+        bias_s,
+        xn_s,
+        qkv_s,
+        sig_s,
+        scores_s,
+        ot_s,
+        send_o,
+        recv_o,
+        ssem,
+        rsem,
+        load_sem,
+    ) = refs[32:]
     group, row, col = (lax.axis_index(name) for name in ("group", "row", "col"))
     big = group * 8 + row
     quad = col // 2
     core = lax.rem(col, 2)
 
+    loads = {
+        name: pltpu.make_async_copy(inputs[name], held[name], load_sem.at[i])
+        for i, name in enumerate(NAMES)
+    }
+    for name in NAMES:
+        loads[name].start()
+
     def on_col(peer):
         return {"col": peer}
 
@@ -149,13 +177,34 @@
 
     swap_in = swap_matrix(True)
     swap_out = swap_matrix(True, transposed=True)
+    pair_ref = held["pair"]
+    wg_ref, wo_ref = held["wg"], held["wo"]
+
+    for name in ("pair", "mask", "wp", "wg", "wo", "gains", "bgain", "bw"):
+        loads[name].wait()
+    proj_weight = [held["wp"][m].T for m in range(2)]
+    gain_in = [held["gains"][m, 0:1, :] for m in range(2)]
+    gain_mid = [
+        jnp.broadcast_to(held["gains"][m, 1:2, :], (128, 128)).T for m in range(2)
+    ]
+    mask = held["mask"][...].astype(F32).astype(BF16)
+    picked = []
+    for lo in range(4):
+        t = lax.broadcasted_iota(jnp.int32, (8, 32), 0)
+        i = lax.broadcasted_iota(jnp.int32, (8, 32), 1)
+        pick = jnp.where(i == t * 4 + lo, 1.0, 0.0).astype(BF16)
+        k = lax.broadcasted_iota(jnp.int32, (32, 128), 0)
+        lane = lax.broadcasted_iota(jnp.int32, (32, 128), 1)
+        place = jnp.where(lane == lo * 32 + k, 1.0, 0.0).astype(BF16)
+        picked.append(mm(mm(pick, mask).astype(BF16), place))
+    mask_flat = picked[0] + picked[1] + picked[2] + picked[3]
 
     def edges(m, state):
         for it in range(8):
-            zn = normalize(state(it), gin_ref[m]).astype(BF16)
+            zn = normalize(state(it), gain_in[m]).astype(BF16)
             gate_s[pl.ds(it * 128, 128), :] = jax.nn.sigmoid(mm(zn, wg_ref[m]))
-            proj = mm(wp_ref[m], zn, NT)
-            keep = mask_ref[it : it + 1, :]
+            proj = mm(proj_weight[m], zn, NT)
+            keep = mask_flat[it : it + 1, :]
             left = keep * jax.nn.sigmoid(proj[0:128]) * proj[128:256]
             right = keep * jax.nn.sigmoid(proj[256:384]) * proj[384:512]
             flat_s[pl.ds(it, 128, stride=16), :] = left
@@ -163,7 +212,7 @@
         for s in range(8):
             send_a[m, s] = flat_s[pl.ds(s * 256, 256), :].astype(BF16)
 
-    def triangle(m):
+    def triangle(m, during_a, during_b):
         go_a = Exchange(
             8,
             quad,
@@ -174,6 +223,7 @@
             rsem.at[5 * m],
         )
         go_a.start()
+        during_a()
         go_a.wait()
         for hi in range(2):
             lanes = jnp.concatenate([recv_a[m, hi * 4 + lo] for lo in range(4)], axis=1)
@@ -190,6 +240,7 @@
             rsem.at[5 * m + 1],
         )
         go_b.start()
+        during_b()
         go_b.wait()
         partner = on_col(quad * 2 + 1 - core)
         cross = remote(
@@ -260,7 +311,7 @@
         nrm_s[...] = (mean_removed * lax.rsqrt(variance + EPS)).reshape(1024, 128)
 
     def update(m, it):
-        normed = (nrm_s[pl.ds(it, 128, stride=8), :] * gmid_ref[m]).astype(BF16)
+        normed = (nrm_s[pl.ds(it, 128, stride=8), :] * gain_mid[m]).astype(BF16)
         return gate_s[pl.ds(it * 128, 128), :] * mm(normed, wo_ref[m], TN)
 
     def first_state(it):
@@ -271,16 +322,38 @@
         z_s[pl.ds(it * 128, 128), :] = z
         return z
 
+    def project(samples):
+        weight = held["watt"][...].reshape(192, 768)
+        for s in samples:
+            for part in range(4):
+                rows = pl.ds(s * 512 + part * 128, 128)
+                value = held["tokens"][rows, :].astype(F32)
+                xn_s[part * 128 : (part + 1) * 128, :] = normalize(
+                    value, held["again"][...].reshape(1, 768)
+                ).astype(BF16)
+            proj = mm(weight, xn_s[...], NT)
+            qkv_s[s] = proj[0:144].astype(BF16)
+            sig_s[s] = jax.nn.sigmoid(proj[144:192])
+            scores_s[s] = mm(qkv_s[s, 0:48, :], qkv_s[s, 48:96, :], TN) * (48.0**-0.5)
+
+    def project_first():
+        for name in ("tokens", "again", "watt"):
+            loads[name].wait()
+        project((0, 1))
+
+    def nothing():
+        pass
+
     edges(0, first_state)
     pl.semaphore_wait(barrier, 30)
-    triangle(0)
+    triangle(0, project_first, lambda: project((2, 3)))
     edges(1, second_state)
-    triangle(1)
+    triangle(1, nothing, nothing)
     for it in range(8):
         z = z_s[pl.ds(it * 128, 128), :] + update(1, it)
         out_ref[pl.ds(it * 128, 128), :] = z
-        zn = normalize(z, bgain_ref[...]).astype(BF16)
-        bias = mm(bw_ref[...], zn, NT).astype(BF16).astype(F32)
+        zn = normalize(z, held["bgain"][...]).astype(BF16)
+        bias = mm(held["bw"][...], zn, NT).astype(BF16).astype(F32)
         heads_s[pl.ds(it, 16, stride=8), :] = bias
     to_head = Exchange(
         16,
@@ -292,6 +365,7 @@
         rsem.at[10],
     )
     to_head.start()
+    swap_plain = swap_matrix(False)
     to_head.wait()
     lanes = jnp.concatenate(
         [
@@ -300,21 +374,21 @@
         ],
         axis=0,
     ).astype(BF16)
-    moved = mm(lanes, swap_matrix(False))
+    moved = mm(lanes, swap_plain)
     for hi in range(4):
         for lo in range(4):
             rows_s[pl.ds(hi * 32 + lo, 8, stride=4), :] = moved[
                 hi * 8 : (hi + 1) * 8, lo * 128 : (lo + 1) * 128
             ]
-    bias_ref[big] = jnp.concatenate(
+    bias_s[big] = jnp.concatenate(
         [rows_s[hi * 32 : (hi + 1) * 32, :] for hi in range(4)], axis=1
     ).astype(BF16)
     spread = Exchange(
         16,
         big,
         on_rows,
-        lambda p: bias_ref.at[big],
-        lambda p: bias_ref.at[p],
+        lambda p: bias_s.at[big],
+        lambda p: bias_s.at[p],
         ssem.at[11],
         rsem.at[11],
     )
@@ -323,27 +397,121 @@
         spread.copy(d).start()
         return carry
 
-    def spread_wait(d, carry):
-        spread.copy(d).wait()
+    to_tokens = Exchange(
+        16,
+        col,
+        on_col,
+        lambda p: send_o.at[p],
+        lambda p: recv_o.at[p],
+        ssem.at[12],
+        rsem.at[12],
+    )
+    lax.fori_loop(1, 16, spread_start, 0)
+
+    def attend(step, carry):
+        part = lax.rem(big // 4 + step, 4)
+        for lo in range(4):
+            source = part * 4 + lo
+
+            @pl.when(source != big)
+            def _():
+                spread.copy(lax.rem(big - source + 16, 16)).wait_recv()
+
+        bias = bias_s[pl.ds(part * 4, 4)].reshape(128, 512).astype(F32)
+        rows = pl.ds(pl.multiple_of(part * 128, 128), 128)
+        for s in range(4):
+            logits = scores_s[s, rows, :] + bias
+            shifted = jnp.exp(logits - jnp.max(logits, axis=-1, keepdims=True))
+            weights = shifted * (1.0 / jnp.sum(shifted, axis=-1, keepdims=True))
+            mixed = mm(qkv_s[s, 96:144, :], weights.astype(BF16), NT)
+            gated = mixed * sig_s[s, :, rows]
+            ot_s[:, s * 128 : (s + 1) * 128] = gated.astype(BF16)
+        moved = mm(ot_s[...], swap_plain).astype(BF16)
+        for lo in range(4):
+            target = part * 4 + lo
+            send_o[target] = moved[:, lo * 128 : (lo + 1) * 128]
+
+            @pl.when(target != col)
+            def _():
+                to_tokens.copy(lax.rem(target - col + 16, 16)).start()
+
+            @pl.when(target == col)
+            def _():
+                to_tokens.own().start()
+
         return carry
 
-    lax.fori_loop(1, 16, spread_start, 0)
-    lax.fori_loop(1, 16, spread_wait, 0)
-
-
-def pair_part(
-    pair, pair_mask, tri_proj, tri_gate, triangle_output_weight, tri_gains, pair_bias_gain, bias_weight
+    lax.fori_loop(0, 4, attend, 0)
+
+    def spread_sent(d, carry):
+        spread.copy(d).wait_send()
+        return carry
+
+    lax.fori_loop(1, 16, spread_sent, 0)
+    for name in ("wout", "tgain", "wup", "wdown"):
+        loads[name].wait()
+    own = [
+        held["tokens"][pl.ds(pl.multiple_of(s * 512 + col * 32, 32), 32), :] for s in range(4)
+    ]
+    own = jnp.concatenate(own, axis=0).astype(F32)
+    to_tokens.wait()
+    first = own + mm(recv_o[...].reshape(768, 128), held["wout"][...], TN)
+    xn2 = normalize(first, held["tgain"][...].reshape(1, 768)).astype(BF16)
+    total = first
+    for j in range(4):
+        up = mm(xn2, held["wup"][:, j * 384 : (j + 1) * 384])
+        side = mm(xn2, held["wup"][:, 1536 + j * 384 : 1536 + (j + 1) * 384])
+        hidden = (jax.nn.silu(up) * side).astype(BF16)
+        total += mm(hidden, held["wdown"][j * 384 : (j + 1) * 384, :])
+    tok_ref[...] = total
+
+
+def on_device(
+    pair,
+    pair_mask,
+    tri_proj,
+    tri_gate,
+    triangle_output_weight,
+    tri_gains,
+    pair_bias_gain,
+    bias_weight,
+    tokens,
+    att_gain,
+    att_proj,
+    att_out,
+    tr_gain,
+    tr_up,
+    tr_down,
 ):
+    operands = (
+        pair.reshape(1024, 128),
+        pair_mask,
+        tri_proj,
+        tri_gate,
+        triangle_output_weight,
+        tri_gains,
+        pair_bias_gain.reshape(1, 128),
+        jnp.swapaxes(bias_weight, 0, 1),
+        tokens.reshape(2048, 768),
+        att_gain,
+        jnp.swapaxes(att_proj, 1, 2),
+        att_out,
+        tr_gain,
+        tr_up,
+        tr_down,
+    )
     vmem = pl.BlockSpec(memory_space=pltpu.VMEM)
-    pair_out, head_bias = pl.pallas_call(
-        pair_kernel,
+    hbm = pl.BlockSpec(memory_space=pl.ANY)
+    pair_out, tokens_out = pl.pallas_call(
+        block_kernel,
         out_shape=(
             jax.ShapeDtypeStruct((1024, 128), F32),
-            jax.ShapeDtypeStruct((16, 32, 512), BF16),
+            jax.ShapeDtypeStruct((128, 768), F32),
         ),
-        in_specs=[vmem] * 9,
+        in_specs=[hbm] * 15,
         out_specs=(vmem, vmem),
-        scratch_shapes=[
+        scratch_shapes=[pltpu.VMEM(x.shape, x.dtype) for x in operands]
+        + [
             pltpu.VMEM((1024, 128), F32),
             pltpu.VMEM((1024, 128), F32),
             pltpu.VMEM((2048, 128), F32),
@@ -361,77 +529,26 @@
             pltpu.VMEM((128, 128), F32),
             pltpu.VMEM((16, 8, 128), F32),
             pltpu.VMEM((128, 128), F32),
-            pltpu.SemaphoreType.DMA((12, 16)),
-            pltpu.SemaphoreType.DMA((12, 16)),
+            pltpu.VMEM((16, 32, 512), BF16),
+            pltpu.VMEM((512, 768), BF16),
+            pltpu.VMEM((4, 144, 512), BF16),
+            pltpu.VMEM((4, 48, 512), F32),
+            pltpu.VMEM((4, 512, 512), F32),
+            pltpu.VMEM((48, 512), BF16),
+            pltpu.VMEM((16, 48, 128), BF16),
+            pltpu.VMEM((16, 48, 128), BF16),
+            pltpu.SemaphoreType.DMA((13, 16)),
+            pltpu.SemaphoreType.DMA((13, 16)),
+            pltpu.SemaphoreType.DMA((15,)),
         ],
         compiler_params=pltpu.CompilerParams(
-            collective_id=0, has_side_effects=True, vmem_limit_bytes=40 * 1024 * 1024
+            collective_id=0, has_side_effects=True, vmem_limit_bytes=60 * 1024 * 1024
         ),
         cost_estimate=pl.CostEstimate(
-            flops=1_500_000_000, bytes_accessed=3_000_000, transcendentals=1_500_000
+            flops=6_000_000_000, bytes_accessed=15_000_000, transcendentals=3_000_000
         ),
-    )(
-        pair.reshape(1024, 128),
-        pair_mask.reshape(8, 128).astype(F32),
-        jnp.swapaxes(tri_proj, 1, 2),
-        tri_gate,
-        triangle_output_weight,
-        tri_gains[:, 0:1, :],
-        jnp.broadcast_to(tri_gains[:, 1, :, None], (2, 128, 128)),
-        pair_bias_gain.reshape(1, 128),
-        jnp.swapaxes(bias_weight, 0, 1),
-    )
-    return pair_out.reshape(32, 32, 128), head_bias.reshape(512, 512)
-
-
-def on_device(
-    pair,
-    pair_mask,
-    tri_proj,
-    tri_gate,
-    triangle_output_weight,
-    tri_gains,
-    pair_bias_gain,
-    bias_weight,
-    tokens,
-    att_gain,
-    att_proj,
-    att_out,
-    tr_gain,
-    tr_up,
-    tr_down,
-):
-    pair_out, head_bias = pair_part(
-        pair,
-        pair_mask,
-        tri_proj,
-        tri_gate,
-        triangle_output_weight,
-        tri_gains,
-        pair_bias_gain,
-        bias_weight,
-    )
-    samples, length, width = tokens.shape
-    head_size = att_proj.shape[2]
-    xn = normalize(tokens.astype(F32), att_gain).astype(BF16)
-    projected = jnp.einsum("snd,fde->fsne", xn, att_proj, preferred_element_type=F32)
-    query, keyed, value = (projected[i].astype(BF16) for i in range(3))
-    scores = jnp.einsum("sqe,ske->sqk", query, keyed, preferred_element_type=F32)
-    scores = scores / jnp.sqrt(F32(head_size)) + head_bias.astype(F32)[None]
-    weights = jax.nn.softmax(scores, axis=-1).astype(BF16)
-    attended = jnp.einsum("sqk,ske->sqe", weights, value, preferred_element_type=F32)
-    attended = (attended * jax.nn.sigmoid(projected[3])).astype(BF16)
-    attended = lax.all_to_all(attended, "col", split_axis=1, concat_axis=2, tiled=True)
-    share = length // lax.axis_size("col")
-    own_tokens = lax.dynamic_slice_in_dim(tokens, lax.axis_index("col") * share, share, 1)
-    mixed = jnp.dot(attended, att_out, preferred_element_type=F32)
-    first = own_tokens.astype(F32) + mixed
-    xn2 = normalize(first, tr_gain).astype(BF16)
-    upped = jnp.dot(xn2, tr_up, preferred_element_type=F32)
-    hidden_width = tr_down.shape[0]
-    hidden = (jax.nn.silu(upped[..., :hidden_width]) * upped[..., hidden_width:]).astype(BF16)
-    tokens_out = first + jnp.dot(hidden, tr_down, preferred_element_type=F32)
-    return (pair_out, tokens_out)
+    )(*operands)
+    return pair_out.reshape(32, 32, 128), tokens_out.reshape(4, 32, 768)
 
 
 def solution(mesh):

time: 173 us -> 131 us (0.76)
  the two profiles are of different devices: /device:TPU:1 before, /device:TPU:27 now
where the time goes in v2:
time: 131 us
  Pallas kernels  127 us (97%)
  local copies, waits for them, and re-layouts  3.64 us (3%)
    pallas_call x1, Pallas kernels, on_device(): pl.pallas_call(block_kernel, out_shape=(jax.ShapeDtypeStruct((1024, 128),...  127 us
    unnamed x2, local copies, waits for them, and re-layouts  3.64 us

profile of v2, /device:TPU:27, one launch (start us, length us, event | category | flops | bytes accessed | tf_op | source)
XLA Modules:
  0.0 131.3 jit_solution(3923221635379879971)
XLA Ops:
  0.6 127.0 %shard_map.158 = (f32[1024,128]{1,0:T(8,128)}, f32[128,768]{1,0:T(8,128)}) custom-call(bf16[1024,128]{1,0:T(8,128)(2,1)} %bitcast.11, s32[32,32]{1,0:T(8,128)} %refs_1_.1, bf16[2,128,512]{2,1,0:T(8,128)(2,1)} %refs_2_.1, bf16[2,128,128]{2,1,0:T(8,128)(2,1)} %refs_3_.1, bf16[2,128,128]{2,1,0:T(8,128)(2,1)} %refs_4_.1, f32[2,2,128]{2,1,0:T(2,128)} %refs_5_.1, ...), custom_call_target="tpu_custom_call" | custom-call | flops 6000000000 | bytes 15000000 | tf_op jit(solution)/shard_map/pallas_call | solution.py:505
  127.6 1.9 %copy.19 = f32[32,32,128]{2,1,0:T(8,128)} copy(f32[32,32,128]{2,1,0:T(8,128)} %bitcast.7) | data formatting | bytes 1048576
  129.5 1.8 %copy.20 = f32[4,32,768]{2,1,0:T(8,128)} copy(f32[4,32,768]{2,1,0:T(8,128)} %bitcast.8) | data formatting | bytes 786432

commit v3 on v2

v3 whole, which is shorter than its diff:
```python
import jax
import jax.numpy as jnp
from jax import lax
from jax.experimental import pallas as pl
from jax.experimental.pallas import tpu as pltpu
from jax.sharding import PartitionSpec as P

EPS = 1e-05
MESH = pl.DeviceIdType.MESH
F32 = jnp.float32
BF16 = jnp.bfloat16
NT = (((1,), (1,)), ((), ()))
TN = (((0,), (0,)), ((), ()))


def normalize(value, gain):
    mean = jnp.mean(value, axis=-1, keepdims=True)
    mean_removed = value - mean
    variance = jnp.mean(mean_removed * mean_removed, axis=-1, keepdims=True)
    return mean_removed * lax.rsqrt(variance + EPS) * gain


def mm(a, b, dims=(((1,), (0,)), ((), ()))):
    return lax.dot_general(a, b, dims, preferred_element_type=F32)


def swap_matrix():
    row = lax.broadcasted_iota(jnp.int32, (512, 512), 0)
    col = lax.broadcasted_iota(jnp.int32, (512, 512), 1)
    a, b, k = row >> 7, (row >> 5) & 3, row & 31
    return jnp.where((b << 7) + (a << 5) + k == col, 1.0, 0.0).astype(BF16)


def remote(src, dst, send, recv, device):
    return pltpu.make_async_remote_copy(
        src_ref=src,
        dst_ref=dst,
        send_sem=send,
        recv_sem=recv,
        device_id=device,
        device_id_type=MESH,
    )


def loop(first, last, step):
    def body(d, carry):
        step(d)
        return carry

    lax.fori_loop(first, last, body, 0)


class Exchange:
    def __init__(self, n, me, device, src, dst, send, recv):
        self.n, self.me, self.device = n, me, device
        self.src, self.dst, self.send, self.recv = src, dst, send, recv

    def copy(self, d):
        peer = lax.rem(self.me + d, self.n)
        return remote(
            self.src(peer), self.dst(self.me), self.send.at[d], self.recv.at[d], self.device(peer)
        )

    def own(self):
        return pltpu.make_async_copy(self.src(self.me), self.dst(self.me), self.recv.at[0])


class Burst:
    def __init__(self, n, me, device, src, dst, all_dst, most_src, send, recv):
        self.n, self.me, self.device = n, me, device
        self.src, self.dst, self.all_dst, self.most_src = src, dst, all_dst, most_src
        self.send, self.recv = send, recv

    def start(self):
        def one(d):
            peer = lax.rem(self.me + d, self.n)
            remote(
                self.src(peer), self.dst(self.me), self.send, self.recv, self.device(peer)
            ).start()

        loop(1, self.n, one)
        pltpu.make_async_copy(self.src(self.me), self.dst(self.me), self.recv).start()

    def wait(self):
        pltpu.make_async_copy(self.all_dst, self.all_dst, self.recv).wait()

    def drain(self):
        pltpu.make_async_copy(self.most_src, self.most_src, self.send).wait()


NAMES = (
    "pair",
    "mask",
    "wp",
    "wg",
    "wo",
    "gains",
    "bgain",
    "bw",
    "tokens",
    "again",
    "watt",
    "wout",
    "tgain",
    "wup",
    "wdown",
)


def block_kernel(*refs):
    inputs = dict(zip(NAMES, refs[:15]))
    out_ref, tok_ref = refs[15:17]
    held = dict(zip(NAMES, refs[17:32]))
    (
        z_s,
        gate_s,
        flat_s,
        nrm_s,
        mix_s,
        wpt_s,
        gmid_s,
        mask_s,
        swap_s,
        send_a,
        recv_a,
        send_b,
        recv_b,
        x_left,
        x_right,
        send_bt,
        recv_bt,
        send_at,
        recv_at,
        heads_s,
        recv_h,
        rows_s,
        bias_s,
        xn_s,
        qkv_s,
        sig_s,
        scores_s,
        ot_s,
        send_o,
        recv_o,
        ssem,
        rsem,
        cross_ssem,
        cross_rsem,
        many_ssem,
        many_rsem,
        load_sem,
    ) = refs[32:]
    group, row, col = (lax.axis_index(name) for name in ("group", "row", "col"))
    big = group * 8 + row
    quad = col // 2
    core = lax.rem(col, 2)

    loads = {
        name: pltpu.make_async_copy(inputs[name], held[name], load_sem.at[i])
        for i, name in enumerate(NAMES)
    }
    for name in NAMES:
        loads[name].start()

    def on_col(peer):
        return {"col": peer}

    def on_quad(peer):
        return {"col": peer * 2 + core}

    def on_rows(peer):
        return {"group": peer // 8, "row": lax.rem(peer, 8)}

    barrier = pltpu.get_barrier_semaphore()

    def greet(d):
        for device in (on_col(lax.rem(col + d, 16)), on_rows(lax.rem(big + d, 16))):
            pl.semaphore_signal(barrier, inc=1, device_id=device, device_id_type=MESH)

    loop(1, 16, greet)

    swap_s[...] = swap_matrix()
    pair_ref = held["pair"]
    wg_ref, wo_ref = held["wg"], held["wo"]

    for name in ("pair", "mask", "wp", "wg", "wo", "gains", "bgain", "bw"):
        loads[name].wait()
    gain_in = [held["gains"][m, 0:1, :] for m in range(2)]
    for m in range(2):
        wpt_s[m] = held["wp"][m].T
        gmid_s[m] = jnp.broadcast_to(held["gains"][m, 1:2, :], (128, 128)).T
    mask = held["mask"][...].astype(F32).astype(BF16)
    picked = []
    for lo in range(4):
        t = lax.broadcasted_iota(jnp.int32, (8, 32), 0)
        i = lax.broadcasted_iota(jnp.int32, (8, 32), 1)
        pick = jnp.where(i == t * 4 + lo, 1.0, 0.0).astype(BF16)
        k = lax.broadcasted_iota(jnp.int32, (32, 128), 0)
        lane = lax.broadcasted_iota(jnp.int32, (32, 128), 1)
        place = jnp.where(lane == lo * 32 + k, 1.0, 0.0).astype(BF16)
        picked.append(mm(mm(pick, mask).astype(BF16), place))
    mask_s[...] = picked[0] + picked[1] + picked[2] + picked[3]

    def edges(m, half, state):
        for t in range(4):
            it = half * 4 + t
            zn = normalize(state(it), gain_in[m]).astype(BF16)
            proj = mm(wpt_s[m], zn, NT)
            keep = mask_s[it : it + 1, :]
            left = keep * jax.nn.sigmoid(proj[0:128]) * proj[128:256]
            right = keep * jax.nn.sigmoid(proj[256:384]) * proj[384:512]
            flat_s[pl.ds(t, 128, stride=8), :] = left
            flat_s[pl.ds(4 + t, 128, stride=8), :] = right
            gate_s[pl.ds(it * 128, 128), :] = jax.nn.sigmoid(mm(zn, wg_ref[m]))
        for s in range(8):
            send_a[m, half, s] = flat_s[pl.ds(s * 128, 128), :].astype(BF16)

    def burst(stage, m, half):
        sems = ssem.at[stage * 4 + m * 2 + half], rsem.at[stage * 4 + m * 2 + half]
        if stage == 0:
            return Burst(
                8,
                quad,
                on_quad,
                lambda p: send_a.at[m, half, p],
                lambda p: recv_a.at[m, half, p],
                recv_a.at[m, half],
                send_a.at[m, half, pl.ds(0, 7)],
                *sems,
            )
        if stage == 1:
            return Burst(
                16,
                big,
                on_rows,
                lambda p: send_b.at[m, half, p],
                lambda p: recv_b.at[m, half, p // 2, lax.rem(p, 2)],
                recv_b.at[m, half],
                send_b.at[m, half, pl.ds(0, 15)],
                *sems,
            )
        if stage == 2:
            return Burst(
                16,
                big,
                on_rows,
                lambda p: send_bt.at[m, half, p],
                lambda p: recv_bt.at[m, half, p],
                recv_bt.at[m, half],
                send_bt.at[m, half, pl.ds(0, 15)],
                *sems,
            )
        return Burst(
            8,
            quad,
            on_quad,
            lambda p: send_at.at[m, half, p],
            lambda p: recv_at.at[m, half, p],
            recv_at.at[m, half],
            send_at.at[m, half, pl.ds(0, 7)],
            *sems,
        )

    partner = on_col(quad * 2 + 1 - core)

    def cross_left(m, half):
        return remote(
            recv_b.at[m, half, :, :, 0],
            x_left.at[m, half],
            cross_ssem.at[m * 2 + half],
            cross_rsem.at[m * 2 + half],
            partner,
        )

    def cross_right(half):
        return remote(
            recv_b.at[0, half, :, 1 - core, 1],
            x_right.at[half],
            cross_ssem.at[4 + half],
            cross_rsem.at[4 + half],
            partner,
        )

    def to_rows(m, half):
        for hi in range(2):
            lanes = jnp.concatenate([recv_a[m, half, hi * 4 + lo] for lo in range(4)], axis=1)
            moved = mm(lanes, swap_s[...])
            for lo in range(4):
                mix_s[pl.ds(hi * 512 + lo, 128, stride=4), :] = moved[:, lo * 128 : (lo + 1) * 128]
        both = jnp.concatenate([mix_s[0:512, :], mix_s[512:1024, :]], axis=1)
        send_b[m, half] = both.astype(BF16).reshape(16, 2, 16, 256)

    def to_channels(m, half):
        for hi in range(2):
            block = recv_bt[m, half, :, :, hi * 128 : (hi + 1) * 128]
            mix_s[hi * 256 : (hi + 1) * 256, :] = block.astype(F32).reshape(256, 128)
        for hi in range(2):
            lanes = jnp.concatenate(
                [mix_s[pl.ds(hi * 256 + lo, 64, stride=4), :] for lo in range(4)], axis=1
            )
            moved = mm(lanes.astype(BF16), swap_s[...]).astype(BF16)
            for lo in range(4):
                send_at[m, half, hi * 4 + lo] = moved[:, lo * 128 : (lo + 1) * 128]

    def triangle(m, gap):
        for half in range(2):
            burst(0, m, half).wait()
            to_rows(m, half)
            burst(1, m, half).start()
        gap()
        for half in range(2):
            burst(0, m, half).drain()
        if m == 0:
            for half in range(2):
                burst(1, m, half).wait()
                cross_left(m, half).start()
                cross_right(half).start()
            right = jnp.concatenate(
                [recv_b[m, half, s, core, 1] for s in range(8) for half in range(2)], axis=0
            )
            own = [mm(recv_b[m, half, :, :, 0].reshape(256, 256), right, NT) for half in range(2)]
            for half in range(2):
                cross_left(m, half).wait_recv()
                cross_right(half).wait_recv()
            right = jnp.concatenate(
                [x_right[half, s] for s in range(8) for half in range(2)], axis=0
            )
            for half in range(2):
                total = own[half] + mm(x_left[m, half].reshape(256, 256), right, NT)
                send_bt[m, half] = total.astype(BF16).reshape(16, 16, 256)
                burst(2, m, half).start()
            for half in range(2):
                cross_right(half).wait_send()
        else:
            right, own = [], None
            for half in range(2):
                burst(1, m, half).wait()
                cross_left(m, half).start()
                right.append(recv_b[m, half, :, :, 1].reshape(256, 256))
                term = mm(recv_b[m, half, :, :, 0].reshape(256, 256), right[half], TN)
                own = term if half == 0 else own + term
            other = None
            for half in range(2):
                cross_left(m, half).wait_recv()
                term = mm(x_left[m, half].reshape(256, 256), right[half], TN)
                other = term if half == 0 else other + term
            for half in range(2):
                for s in range(8):
                    at = slice(s * 32 + half * 16, s * 32 + half * 16 + 16)
                    send_bt[m, half, s * 2 + core] = own[at].astype(BF16)
                    send_bt[m, half, s * 2 + 1 - core] = other[at].astype(BF16)
                burst(2, m, half).start()
        for half in range(2):
            burst(1, m, half).drain()
            cross_left(m, half).wait_send()
        for half in range(2):
            burst(2, m, half).wait()
            to_channels(m, half)
            burst(3, m, half).start()
        for half in range(2):
            burst(2, m, half).drain()

    def middle_norm(m, half):
        summed = recv_at[m, half].astype(F32).reshape(64, 8, 128)

        def over_channels(value):
            pairs = jnp.sum(value, axis=0)
            return (pairs + pltpu.roll(pairs, 4, 0)) * (1.0 / 128)

        mean_removed = summed - over_channels(summed)[None]
        variance = over_channels(mean_removed * mean_removed)
        nrm_s[...] = (mean_removed * lax.rsqrt(variance + EPS)[None]).reshape(512, 128)

    def update(m, it):
        normed = (nrm_s[pl.ds(it % 4, 128, stride=4), :] * gmid_s[m]).astype(BF16)
        return gate_s[pl.ds(it * 128, 128), :] * mm(normed, wo_ref[m], TN)

    def first_state(it):
        return pair_ref[pl.ds(it * 128, 128), :].astype(F32)

    def second_state(it):
        z = first_state(it) + update(0, it)
        z_s[pl.ds(it * 128, 128), :] = z
        return z

    def project(samples):
        weight = held["watt"][...].reshape(192, 768)
        for s in samples:
            for part in range(4):
                rows = pl.ds(s * 512 + part * 128, 128)
                value = held["tokens"][rows, :].astype(F32)
                xn_s[part * 128 : (part + 1) * 128, :] = normalize(
                    value, held["again"][...].reshape(1, 768)
                ).astype(BF16)
            proj = mm(weight, xn_s[...], NT)
            qkv_s[s] = proj[0:144].astype(BF16)
            sig_s[s] = jax.nn.sigmoid(proj[144:192])
            scores_s[s] = mm(qkv_s[s, 0:48, :], qkv_s[s, 48:96, :], TN) * (48.0**-0.5)

    def gap_first():
        for name in ("tokens", "again", "watt"):
            loads[name].wait()
        project((0, 1))

    edges(0, 0, first_state)
    pl.semaphore_wait(barrier, 30)
    burst(0, 0, 0).start()
    edges(0, 1, first_state)
    burst(0, 0, 1).start()
    triangle(0, gap_first)
    for half in range(2):
        burst(3, 0, half).wait()
        middle_norm(0, half)
        edges(1, half, second_state)
        burst(0, 1, half).start()
    for half in range(2):
        burst(3, 0, half).drain()
    triangle(1, lambda: project((2, 3)))
    for half in range(2):
        burst(3, 1, half).wait()
        middle_norm(1, half)
        for it in range(half * 4, half * 4 + 4):
            z = z_s[pl.ds(it * 128, 128), :] + update(1, it)
            out_ref[pl.ds(it * 128, 128), :] = z
            zn = normalize(z, held["bgain"][...]).astype(BF16)
            bias = mm(held["bw"][...], zn, NT).astype(BF16).astype(F32)
            heads_s[pl.ds(it, 16, stride=8), :] = bias
    to_head = Burst(
        16,
        col,
        on_col,
        lambda p: heads_s.at[pl.ds(p * 8, 8)],
        lambda p: recv_h.at[p],
        recv_h,
        heads_s.at[pl.ds(0, 120)],
        ssem.at[16],
        rsem.at[16],
    )
    to_head.start()
    for half in range(2):
        burst(3, 1, half).drain()
    to_head.wait()
    lanes = jnp.concatenate(
        [
            jnp.concatenate([recv_h[hi * 4 + lo] for lo in range(4)], axis=1)
            for hi in range(4)
        ],
        axis=0,
    ).astype(BF16)
    moved = mm(lanes, swap_s[...])
    for hi in range(4):
        for lo in range(4):
            rows_s[pl.ds(hi * 32 + lo, 8, stride=4), :] = moved[
                hi * 8 : (hi + 1) * 8, lo * 128 : (lo + 1) * 128
            ]
    bias_s[big] = jnp.concatenate(
        [rows_s[hi * 32 : (hi + 1) * 32, :] for hi in range(4)], axis=1
    ).astype(BF16)
    spread = Exchange(
        16,
        big,
        on_rows,
        lambda p: bias_s.at[big],
        lambda p: bias_s.at[p],
        many_ssem.at[0],
        many_rsem.at[0],
    )

    to_tokens = Exchange(
        16,
        col,
        on_col,
        lambda p: send_o.at[p],
        lambda p: recv_o.at[p],
        many_ssem.at[1],
        many_rsem.at[1],
    )
    loop(1, 16, lambda d: spread.copy(d).start())

    def attend(step, carry):
        part = lax.rem(big // 4 + step, 4)
        for lo in range(4):
            source = part * 4 + lo

            @pl.when(source != big)
            def _():
                spread.copy(lax.rem(big - source + 16, 16)).wait_recv()

        bias = bias_s[pl.ds(part * 4, 4)].reshape(128, 512).astype(F32)
        rows = pl.ds(pl.multiple_of(part * 128, 128), 128)
        for s in range(4):
            logits = scores_s[s, rows, :] + bias
            shifted = jnp.exp(logits - jnp.max(logits, axis=-1, keepdims=True))
            weights = shifted * (1.0 / jnp.sum(shifted, axis=-1, keepdims=True))
            mixed = mm(qkv_s[s, 96:144, :], weights.astype(BF16), NT)
            gated = mixed * sig_s[s, :, rows]
            ot_s[:, s * 128 : (s + 1) * 128] = gated.astype(BF16)
        moved = mm(ot_s[...], swap_s[...]).astype(BF16)
        for lo in range(4):
            target = part * 4 + lo
            send_o[target] = moved[:, lo * 128 : (lo + 1) * 128]

            @pl.when(target != col)
            def _():
                to_tokens.copy(lax.rem(target - col + 16, 16)).start()

            @pl.when(target == col)
            def _():
                to_tokens.own().start()

        return carry

    lax.fori_loop(0, 4, attend, 0)

    loop(1, 16, lambda d: spread.copy(d).wait_send())
    to_head.drain()
    for name in ("wout", "tgain", "wup", "wdown"):
        loads[name].wait()
    own = [
        held["tokens"][pl.ds(pl.multiple_of(s * 512 + col * 32, 32), 32), :] for s in range(4)
    ]
    own = jnp.concatenate(own, axis=0).astype(F32)
    to_tokens.own().wait()
    loop(1, 16, lambda d: to_tokens.copy(d).wait())
    first = own + mm(recv_o[...].reshape(768, 128), held["wout"][...], TN)
    xn2 = normalize(first, held["tgain"][...].reshape(1, 768)).astype(BF16)
    total = first
    for j in range(4):
        up = mm(xn2, held["wup"][:, j * 384 : (j + 1) * 384])
        side = mm(xn2, held["wup"][:, 1536 + j * 384 : 1536 + (j + 1) * 384])
        hidden = (jax.nn.silu(up) * side).astype(BF16)
        total += mm(hidden, held["wdown"][j * 384 : (j + 1) * 384, :])
    tok_ref[...] = total


def on_device(
    pair,
    pair_mask,
    tri_proj,
    tri_gate,
    triangle_output_weight,
    tri_gains,
    pair_bias_gain,
    bias_weight,
    tokens,
    att_gain,
    att_proj,
    att_out,
    tr_gain,
    tr_up,
    tr_down,
):
    operands = (
        pair.reshape(1024, 128),
        pair_mask,
        tri_proj,
        tri_gate,
        triangle_output_weight,
        tri_gains,
        pair_bias_gain.reshape(1, 128),
        jnp.swapaxes(bias_weight, 0, 1),
        tokens.reshape(2048, 768),
        att_gain,
        jnp.swapaxes(att_proj, 1, 2),
        att_out,
        tr_gain,
        tr_up,
        tr_down,
    )
    vmem = pl.BlockSpec(memory_space=pltpu.VMEM)
    hbm = pl.BlockSpec(memory_space=pl.ANY)
    pair_out, tokens_out = pl.pallas_call(
        block_kernel,
        out_shape=(
            jax.ShapeDtypeStruct((1024, 128), F32),
            jax.ShapeDtypeStruct((128, 768), F32),
        ),
        in_specs=[hbm] * 15,
        out_specs=(vmem, vmem),
        scratch_shapes=[pltpu.VMEM(x.shape, x.dtype) for x in operands]
        + [
            pltpu.VMEM((1024, 128), F32),
            pltpu.VMEM((1024, 128), F32),
            pltpu.VMEM((1024, 128), F32),
            pltpu.VMEM((512, 128), F32),
            pltpu.VMEM((1024, 128), F32),
            pltpu.VMEM((2, 512, 128), BF16),
            pltpu.VMEM((2, 128, 128), F32),
            pltpu.VMEM((8, 128), F32),
            pltpu.VMEM((512, 512), BF16),
            pltpu.VMEM((2, 2, 8, 128, 128), BF16),
            pltpu.VMEM((2, 2, 8, 128, 128), BF16),
            pltpu.VMEM((2, 2, 16, 2, 16, 256), BF16),
            pltpu.VMEM((2, 2, 8, 2, 2, 16, 256), BF16),
            pltpu.VMEM((2, 2, 8, 2, 16, 256), BF16),
            pltpu.VMEM((2, 8, 16, 256), BF16),
            pltpu.VMEM((2, 2, 16, 16, 256), BF16),
            pltpu.VMEM((2, 2, 16, 16, 256), BF16),
            pltpu.VMEM((2, 2, 8, 64, 128), BF16),
            pltpu.VMEM((2, 2, 8, 64, 128), BF16),
            pltpu.VMEM((128, 128), F32),
            pltpu.VMEM((16, 8, 128), F32),
            pltpu.VMEM((128, 128), F32),
            pltpu.VMEM((16, 32, 512), BF16),
            pltpu.VMEM((512, 768), BF16),
            pltpu.VMEM((4, 144, 512), BF16),
            pltpu.VMEM((4, 48, 512), F32),
            pltpu.VMEM((4, 512, 512), F32),
            pltpu.VMEM((48, 512), BF16),
            pltpu.VMEM((16, 48, 128), BF16),
            pltpu.VMEM((16, 48, 128), BF16),
            pltpu.SemaphoreType.DMA((17,)),
            pltpu.SemaphoreType.DMA((17,)),
            pltpu.SemaphoreType.DMA((6,)),
            pltpu.SemaphoreType.DMA((6,)),
            pltpu.SemaphoreType.DMA((2, 16)),
            pltpu.SemaphoreType.DMA((2, 16)),
            pltpu.SemaphoreType.DMA((15,)),
        ],
        compiler_params=pltpu.CompilerParams(
            collective_id=0, has_side_effects=True, vmem_limit_bytes=60 * 1024 * 1024
        ),
        cost_estimate=pl.CostEstimate(
            flops=6_000_000_000, bytes_accessed=15_000_000, transcendentals=3_000_000
        ),
    )(*operands)
    return pair_out.reshape(32, 32, 128), tokens_out.reshape(4, 32, 768)


def solution(mesh):
    placed = (
        P(("group", "row"), "col", None),
        P(("group", "row"), "col"),
        P(),
        P(),
        P(),
        P(),
        P(),
        P(),
        P(("group", "row"), None, None),
        P(),
        P(None, None, "col"),
        P(),
        P(),
        P(),
        P(),
    )
    return jax.shard_map(
        on_device,
        mesh=mesh,
        in_specs=placed,
        out_specs=(P(("group", "row"), "col", None), P(("group", "row"), "col", None)),
        check_vma=False,
    )
```

time: 131 us -> 118 us (0.901); the launches traced: 131 us -> 116 us
  Pallas kernels: 127 us -> 112 us
    pallas_call x1, Pallas kernels: 127 us -> 112 us  [on_device(): pl.pallas_call(block_kernel, out_shape=(jax.ShapeDtypeStruct((1024, 128),...]
where the time goes in v3:
time: 118 us; the launch traced here: 116 us
  Pallas kernels  112 us (95%)
  local copies, waits for them, and re-layouts  3.64 us (3%)
    pallas_call x1, Pallas kernels, on_device(): pl.pallas_call(block_kernel, out_shape=(jax.ShapeDtypeStruct((1024, 128),...  112 us
    unnamed x2, local copies, waits for them, and re-layouts  3.64 us

profile of v3, /device:TPU:27, one launch (start us, length us, event | category | flops | bytes accessed | tf_op | source)
XLA Modules:
  0.0 116.4 jit_solution(4440748096479518792)
XLA Ops:
  0.6 112.1 %shard_map.158 = (f32[1024,128]{1,0:T(8,128)}, f32[128,768]{1,0:T(8,128)}) custom-call(bf16[1024,128]{1,0:T(8,128)(2,1)} %bitcast.11, s32[32,32]{1,0:T(8,128)} %refs_1_.1, bf16[2,128,512]{2,1,0:T(8,128)(2,1)} %refs_2_.1, bf16[2,128,128]{2,1,0:T(8,128)(2,1)} %refs_3_.1, bf16[2,128,128]{2,1,0:T(8,128)(2,1)} %refs_4_.1, f32[2,2,128]{2,1,0:T(2,128)} %refs_5_.1, ...), custom_call_target="tpu_custom_call" | custom-call | flops 6000000000 | bytes 15000000 | tf_op jit(solution)/shard_map/pallas_call | solution.py:572
  112.7 1.9 %copy.19 = f32[32,32,128]{2,1,0:T(8,128)} copy(f32[32,32,128]{2,1,0:T(8,128)} %bitcast.7) | data formatting | bytes 1048576
  114.6 1.8 %copy.20 = f32[4,32,768]{2,1,0:T(8,128)} copy(f32[4,32,768]{2,1,0:T(8,128)} %bitcast.8) | data formatting | bytes 786432

commit v4 on v3

--- a/solution.py
+++ b/solution.py
@@ -65,20 +65,32 @@
         return pltpu.make_async_copy(self.src(self.me), self.dst(self.me), self.recv.at[0])
 
 
+def ring(at, i, n):
+    step = (i + 1) // 2
+    return lax.rem(at + jnp.where(lax.rem(i, 2) == 1, step, n - step), n)
+
+
 class Burst:
-    def __init__(self, n, me, device, src, dst, all_dst, most_src, send, recv):
-        self.n, self.me, self.device = n, me, device
+    def __init__(self, n, at, pair, device, src, dst, all_dst, most_src, send, recv):
+        self.n, self.at, self.pair, self.me, self.device = n, at, pair, pair * n + at, device
         self.src, self.dst, self.all_dst, self.most_src = src, dst, all_dst, most_src
         self.send, self.recv = send, recv
 
+    def to(self, peer):
+        remote(
+            self.src(peer), self.dst(self.me), self.send, self.recv, self.device(peer)
+        ).start()
+
     def start(self):
-        def one(d):
-            peer = lax.rem(self.me + d, self.n)
-            remote(
-                self.src(peer), self.dst(self.me), self.send, self.recv, self.device(peer)
-            ).start()
-
-        loop(1, self.n, one)
+        other = 1 - self.pair
+
+        def both(j):
+            place = ring(self.at, self.n - 1 - j, self.n)
+            self.to(other * self.n + place)
+            self.to(self.pair * self.n + place)
+
+        loop(0, self.n - 1, both)
+        self.to(other * self.n + self.at)
         pltpu.make_async_copy(self.src(self.me), self.dst(self.me), self.recv).start()
 
     def wait(self):
@@ -219,8 +231,9 @@
         sems = ssem.at[stage * 4 + m * 2 + half], rsem.at[stage * 4 + m * 2 + half]
         if stage == 0:
             return Burst(
-                8,
-                quad,
+                4,
+                lax.rem(quad, 4),
+                quad // 4,
                 on_quad,
                 lambda p: send_a.at[m, half, p],
                 lambda p: recv_a.at[m, half, p],
@@ -230,8 +243,9 @@
             )
         if stage == 1:
             return Burst(
-                16,
-                big,
+                8,
+                row,
+                group,
                 on_rows,
                 lambda p: send_b.at[m, half, p],
                 lambda p: recv_b.at[m, half, p // 2, lax.rem(p, 2)],
@@ -241,8 +255,9 @@
             )
         if stage == 2:
             return Burst(
-                16,
-                big,
+                8,
+                row,
+                group,
                 on_rows,
                 lambda p: send_bt.at[m, half, p],
                 lambda p: recv_bt.at[m, half, p],
@@ -251,8 +266,9 @@
                 *sems,
             )
         return Burst(
-            8,
-            quad,
+            4,
+            lax.rem(quad, 4),
+            quad // 4,
             on_quad,
             lambda p: send_at.at[m, half, p],
             lambda p: recv_at.at[m, half, p],
@@ -426,8 +442,9 @@
             bias = mm(held["bw"][...], zn, NT).astype(BF16).astype(F32)
             heads_s[pl.ds(it, 16, stride=8), :] = bias
     to_head = Burst(
-        16,
-        col,
+        8,
+        lax.rem(col, 8),
+        col // 8,
         on_col,
         lambda p: heads_s.at[pl.ds(p * 8, 8)],
         lambda p: recv_h.at[p],
@@ -456,16 +473,27 @@
     bias_s[big] = jnp.concatenate(
         [rows_s[hi * 32 : (hi + 1) * 32, :] for hi in range(4)], axis=1
     ).astype(BF16)
-    spread = Exchange(
-        16,
-        big,
-        on_rows,
-        lambda p: bias_s.at[big],
-        lambda p: bias_s.at[p],
-        many_ssem.at[0],
-        many_rsem.at[0],
-    )
-
+    def along(offset):
+        return remote(
+            bias_s.at[big],
+            bias_s.at[big],
+            many_ssem.at[0, offset],
+            many_rsem.at[0, offset],
+            {"row": lax.rem(row + offset, 8)},
+        )
+
+    def across(owner, z):
+        return remote(
+            bias_s.at[owner * 8 + z],
+            bias_s.at[owner * 8 + z],
+            many_ssem.at[0, 8 + z],
+            many_rsem.at[0, 8 + z],
+            {"group": 1 - group},
+        )
+
+    across(group, row).start()
+    for offset in (4, 3, 5, 2, 6, 1, 7):
+        along(offset).start()
     to_tokens = Exchange(
         16,
         col,
@@ -475,16 +503,22 @@
         many_ssem.at[1],
         many_rsem.at[1],
     )
-    loop(1, 16, lambda d: spread.copy(d).start())
 
     def attend(step, carry):
-        part = lax.rem(big // 4 + step, 4)
+        owner = lax.rem(group + step // 2, 2)
+        side = lax.rem(row // 4 + step, 2)
+        part = owner * 2 + side
         for lo in range(4):
-            source = part * 4 + lo
-
-            @pl.when(source != big)
+            z = side * 4 + lo
+
+            @pl.when(jnp.logical_and(step < 2, z != row))
             def _():
-                spread.copy(lax.rem(big - source + 16, 16)).wait_recv()
+                along(lax.rem(row - z + 8, 8)).wait_recv()
+                across(owner, z).start()
+
+            @pl.when(step >= 2)
+            def _():
+                across(owner, z).wait_recv()
 
         bias = bias_s[pl.ds(part * 4, 4)].reshape(128, 512).astype(F32)
         rows = pl.ds(pl.multiple_of(part * 128, 128), 128)
@@ -512,7 +546,8 @@
 
     lax.fori_loop(0, 4, attend, 0)
 
-    loop(1, 16, lambda d: spread.copy(d).wait_send())
+    loop(1, 8, lambda d: along(d).wait_send())
+    loop(0, 8, lambda z: across(group, z).wait_send())
     to_head.drain()
     for name in ("wout", "tgain", "wup", "wdown"):
         loads[name].wait()
@@ -531,6 +566,21 @@
         hidden = (jax.nn.silu(up) * side).astype(BF16)
         total += mm(hidden, held["wdown"][j * 384 : (j + 1) * 384, :])
     tok_ref[...] = total
+
+
+def close_kernel(pair_ref, tokens_ref, pair_out, tokens_out, sem):
+    copies = []
+    for i in range(4):
+        rows = pl.ds(i * 256, 256)
+        copies.append(pltpu.make_async_copy(pair_ref.at[rows], pair_out.at[rows], sem.at[i]))
+        rows = pl.ds(i * 32, 32)
+        copies.append(
+            pltpu.make_async_copy(tokens_ref.at[rows], tokens_out.at[rows], sem.at[4 + i])
+        )
+    for copy in copies:
+        copy.start()
+    for copy in copies:
+        copy.wait()
 
 
 def on_device(
@@ -624,6 +674,16 @@
             flops=6_000_000_000, bytes_accessed=15_000_000, transcendentals=3_000_000
         ),
     )(*operands)
+    pair_out, tokens_out = pl.pallas_call(
+        close_kernel,
+        out_shape=(
+            jax.ShapeDtypeStruct((1024, 128), F32),
+            jax.ShapeDtypeStruct((128, 768), F32),
+        ),
+        in_specs=[hbm, hbm],
+        out_specs=(hbm, hbm),
+        scratch_shapes=[pltpu.SemaphoreType.DMA((8,))],
+    )(pair_out, tokens_out)
     return pair_out.reshape(32, 32, 128), tokens_out.reshape(4, 32, 768)
 
 

time: 118 us -> 137 us (1.16); the launches traced: 116 us -> 137 us
  Pallas kernels: 112 us -> 136 us
  local copies, waits for them, and re-layouts: 3.64 us -> 0 us
    pallas_call x0 -> x1, Pallas kernels: none -> 29 us  [on_device(): pl.pallas_call(close_kernel, out_shape=(jax.ShapeDtypeStruct((1024, 128),...]
    pallas_call x1, Pallas kernels: 112 us -> 107 us  [on_device(): pl.pallas_call(block_kernel, out_shape=(jax.ShapeDtypeStruct((1024, 128),...]
    unnamed x2 -> x0, local copies, waits for them, and re-layouts: 3.64 us -> none
where the time goes in v4:
time: 137 us
  Pallas kernels  136 us (99%)
    pallas_call x1, Pallas kernels, on_device(): pl.pallas_call(block_kernel, out_shape=(jax.ShapeDtypeStruct((1024, 128),...  107 us
    pallas_call x1, Pallas kernels, on_device(): pl.pallas_call(close_kernel, out_shape=(jax.ShapeDtypeStruct((1024, 128),...  29 us

profile of v4, /device:TPU:27, one launch (start us, length us, event | category | flops | bytes accessed | tf_op | source)
XLA Modules:
  0.0 136.8 jit_solution(5556565611718429700)
XLA Ops:
  0.6 107.1 %shard_map.158 = (f32[1024,128]{1,0:T(8,128)}, f32[128,768]{1,0:T(8,128)}) custom-call(bf16[1024,128]{1,0:T(8,128)(2,1)} %bitcast.11, s32[32,32]{1,0:T(8,128)} %refs_1_.1, bf16[2,128,512]{2,1,0:T(8,128)(2,1)} %refs_2_.1, bf16[2,128,128]{2,1,0:T(8,128)(2,1)} %refs_3_.1, bf16[2,128,128]{2,1,0:T(8,128)(2,1)} %refs_4_.1, f32[2,2,128]{2,1,0:T(2,128)} %refs_5_.1, ...), custom_call_target="tpu_custom_call" | custom-call | flops 6000000000 | bytes 15000000 | tf_op jit(solution)/shard_map/pallas_call | solution.py:622
  107.8 29.0 %shard_map.159 = (f32[1024,128]{1,0:T(8,128)}, f32[128,768]{1,0:T(8,128)}) custom-call(f32[1024,128]{1,0:T(8,128)} %get-tuple-element.6.pair_ref, f32[128,768]{1,0:T(8,128)} %get-tuple-element.7.tokens_ref), custom_call_target="tpu_custom_call" | custom-call | tf_op jit(solution)/shard_map/pallas_call | solution.py:677

commit v5 on v4

--- a/solution.py
+++ b/solution.py
@@ -65,33 +65,38 @@
         return pltpu.make_async_copy(self.src(self.me), self.dst(self.me), self.recv.at[0])
 
 
-def ring(at, i, n):
-    step = (i + 1) // 2
-    return lax.rem(at + jnp.where(lax.rem(i, 2) == 1, step, n - step), n)
+def ring(at, n):
+    steps = [n // 2]
+    for step in range(n // 2 - 1, 0, -1):
+        steps += [step, n - step]
+    return [lax.rem(at + step, n) for step in steps]
+
+
+def sigmoid(value):
+    return 0.5 * jnp.tanh(0.5 * value) + 0.5
 
 
 class Burst:
-    def __init__(self, n, at, pair, device, src, dst, all_dst, most_src, send, recv):
-        self.n, self.at, self.pair, self.me, self.device = n, at, pair, pair * n + at, device
+    def __init__(self, n, places, at, pair, device, src, dst, all_dst, most_src, send, recv):
+        self.n, self.places, self.at, self.pair = n, places, at, pair
+        self.device = device
         self.src, self.dst, self.all_dst, self.most_src = src, dst, all_dst, most_src
         self.send, self.recv = send, recv
 
-    def to(self, peer):
-        remote(
-            self.src(peer), self.dst(self.me), self.send, self.recv, self.device(peer)
-        ).start()
-
     def start(self):
-        other = 1 - self.pair
-
-        def both(j):
-            place = ring(self.at, self.n - 1 - j, self.n)
-            self.to(other * self.n + place)
-            self.to(self.pair * self.n + place)
-
-        loop(0, self.n - 1, both)
-        self.to(other * self.n + self.at)
-        pltpu.make_async_copy(self.src(self.me), self.dst(self.me), self.recv).start()
+        me, other = self.pair * self.n + self.at, 1 - self.pair
+        for place in self.places + [self.at]:
+            for pair in (other, self.pair):
+                if place is self.at and pair is self.pair:
+                    continue
+                remote(
+                    self.src(pair * self.n + place),
+                    self.dst(me),
+                    self.send,
+                    self.recv,
+                    self.device(pair, place),
+                ).start()
+        pltpu.make_async_copy(self.src(me), self.dst(me), self.recv).start()
 
     def wait(self):
         pltpu.make_async_copy(self.all_dst, self.all_dst, self.recv).wait()
@@ -164,7 +169,7 @@
     ) = refs[32:]
     group, row, col = (lax.axis_index(name) for name in ("group", "row", "col"))
     big = group * 8 + row
-    quad = col // 2
+    quad = lax.div(col, 2)
     core = lax.rem(col, 2)
 
     loads = {
@@ -177,16 +182,24 @@
     def on_col(peer):
         return {"col": peer}
 
-    def on_quad(peer):
-        return {"col": peer * 2 + core}
-
-    def on_rows(peer):
-        return {"group": peer // 8, "row": lax.rem(peer, 8)}
+    def on_quad(pair, place):
+        return {"col": pair * 8 + place * 2 + core}
+
+    def on_rows(pair, place):
+        return {"group": pair, "row": place}
+
+    row_ring = ring(row, 8)
+    quad_at, quad_pair = lax.rem(quad, 4), lax.div(quad, 4)
+    quad_ring = ring(quad_at, 4)
 
     barrier = pltpu.get_barrier_semaphore()
 
     def greet(d):
-        for device in (on_col(lax.rem(col + d, 16)), on_rows(lax.rem(big + d, 16))):
+        place = lax.rem(big + d, 16)
+        for device in (
+            on_col(lax.rem(col + d, 16)),
+            on_rows(lax.div(place, 8), lax.rem(place, 8)),
+        ):
             pl.semaphore_signal(barrier, inc=1, device_id=device, device_id_type=MESH)
 
     loop(1, 16, greet)
@@ -214,16 +227,19 @@
     mask_s[...] = picked[0] + picked[1] + picked[2] + picked[3]
 
     def edges(m, half, state):
-        for t in range(4):
-            it = half * 4 + t
-            zn = normalize(state(it), gain_in[m]).astype(BF16)
+        for two in range(2):
+            it = half * 4 + two * 2
+            z = jnp.concatenate([state(it), state(it + 1)], axis=0)
+            zn = normalize(z, gain_in[m]).astype(BF16)
             proj = mm(wpt_s[m], zn, NT)
-            keep = mask_s[it : it + 1, :]
-            left = keep * jax.nn.sigmoid(proj[0:128]) * proj[128:256]
-            right = keep * jax.nn.sigmoid(proj[256:384]) * proj[384:512]
-            flat_s[pl.ds(t, 128, stride=8), :] = left
-            flat_s[pl.ds(4 + t, 128, stride=8), :] = right
-            gate_s[pl.ds(it * 128, 128), :] = jax.nn.sigmoid(mm(zn, wg_ref[m]))
+            for t in range(2):
+                part = proj[:, t * 128 : (t + 1) * 128]
+                keep = mask_s[it + t : it + t + 1, :]
+                left = keep * sigmoid(part[0:128]) * part[128:256]
+                right = keep * sigmoid(part[256:384]) * part[384:512]
+                flat_s[pl.ds(two * 2 + t, 128, stride=8), :] = left
+                flat_s[pl.ds(4 + two * 2 + t, 128, stride=8), :] = right
+            gate_s[pl.ds(it * 128, 256), :] = sigmoid(mm(zn, wg_ref[m]))
         for s in range(8):
             send_a[m, half, s] = flat_s[pl.ds(s * 128, 128), :].astype(BF16)
 
@@ -232,8 +248,9 @@
         if stage == 0:
             return Burst(
                 4,
-                lax.rem(quad, 4),
-                quad // 4,
+                quad_ring,
+                quad_at,
+                quad_pair,
                 on_quad,
                 lambda p: send_a.at[m, half, p],
                 lambda p: recv_a.at[m, half, p],
@@ -244,11 +261,12 @@
         if stage == 1:
             return Burst(
                 8,
+                row_ring,
                 row,
                 group,
                 on_rows,
                 lambda p: send_b.at[m, half, p],
-                lambda p: recv_b.at[m, half, p // 2, lax.rem(p, 2)],
+                lambda p: recv_b.at[m, half, lax.div(p, 2), lax.rem(p, 2)],
                 recv_b.at[m, half],
                 send_b.at[m, half, pl.ds(0, 15)],
                 *sems,
@@ -256,6 +274,7 @@
         if stage == 2:
             return Burst(
                 8,
+                row_ring,
                 row,
                 group,
                 on_rows,
@@ -267,8 +286,9 @@
             )
         return Burst(
             4,
-            lax.rem(quad, 4),
-            quad // 4,
+            quad_ring,
+            quad_at,
+            quad_pair,
             on_quad,
             lambda p: send_at.at[m, half, p],
             lambda p: recv_at.at[m, half, p],
@@ -410,7 +430,7 @@
                 ).astype(BF16)
             proj = mm(weight, xn_s[...], NT)
             qkv_s[s] = proj[0:144].astype(BF16)
-            sig_s[s] = jax.nn.sigmoid(proj[144:192])
+            sig_s[s] = sigmoid(proj[144:192])
             scores_s[s] = mm(qkv_s[s, 0:48, :], qkv_s[s, 48:96, :], TN) * (48.0**-0.5)
 
     def gap_first():
@@ -443,9 +463,10 @@
             heads_s[pl.ds(it, 16, stride=8), :] = bias
     to_head = Burst(
         8,
+        ring(lax.rem(col, 8), 8),
         lax.rem(col, 8),
-        col // 8,
-        on_col,
+        lax.div(col, 8),
+        lambda pair, place: on_col(pair * 8 + place),
         lambda p: heads_s.at[pl.ds(p * 8, 8)],
         lambda p: recv_h.at[p],
         recv_h,
@@ -563,24 +584,31 @@
     for j in range(4):
         up = mm(xn2, held["wup"][:, j * 384 : (j + 1) * 384])
         side = mm(xn2, held["wup"][:, 1536 + j * 384 : 1536 + (j + 1) * 384])
-        hidden = (jax.nn.silu(up) * side).astype(BF16)
+        hidden = (up * sigmoid(up) * side).astype(BF16)
         total += mm(hidden, held["wdown"][j * 384 : (j + 1) * 384, :])
     tok_ref[...] = total
 
 
-def close_kernel(pair_ref, tokens_ref, pair_out, tokens_out, sem):
+def close_kernel(pair_ref, tokens_ref, pair_out, tokens_out, pair_s, tokens_s, in_sem, out_sem):
     copies = []
     for i in range(4):
-        rows = pl.ds(i * 256, 256)
-        copies.append(pltpu.make_async_copy(pair_ref.at[rows], pair_out.at[rows], sem.at[i]))
-        rows = pl.ds(i * 32, 32)
-        copies.append(
-            pltpu.make_async_copy(tokens_ref.at[rows], tokens_out.at[rows], sem.at[4 + i])
-        )
-    for copy in copies:
-        copy.start()
-    for copy in copies:
-        copy.wait()
+        for n, (src, held, dst, size) in enumerate(
+            ((pair_ref, pair_s, pair_out, 256), (tokens_ref, tokens_s, tokens_out, 32))
+        ):
+            rows = pl.ds(i * size, size)
+            copies.append(
+                (
+                    pltpu.make_async_copy(src.at[rows], held.at[rows], in_sem.at[n, i]),
+                    pltpu.make_async_copy(held.at[rows], dst.at[rows], out_sem.at[n, i]),
+                )
+            )
+    for first, _ in copies:
+        first.start()
+    for first, second in copies:
+        first.wait()
+        second.start()
+    for _, second in copies:
+        second.wait()
 
 
 def on_device(
@@ -682,7 +710,13 @@
         ),
         in_specs=[hbm, hbm],
         out_specs=(hbm, hbm),
-        scratch_shapes=[pltpu.SemaphoreType.DMA((8,))],
+        scratch_shapes=[
+            pltpu.VMEM((1024, 128), F32),
+            pltpu.VMEM((128, 768), F32),
+            pltpu.SemaphoreType.DMA((2, 4)),
+            pltpu.SemaphoreType.DMA((2, 4)),
+        ],
+        compiler_params=pltpu.CompilerParams(vmem_limit_bytes=60 * 1024 * 1024),
     )(pair_out, tokens_out)
     return pair_out.reshape(32, 32, 128), tokens_out.reshape(4, 32, 768)
 

time: 137 us -> 111 us (0.81)
  Pallas kernels: 136 us -> 110 us
    pallas_call x1, Pallas kernels: 29 us -> 2.05 us  [on_device(): pl.pallas_call(close_kernel, out_shape=(jax.ShapeDtypeStruct((1024, 128),...]
where the time goes in v5:
time: 111 us
  Pallas kernels  110 us (99%)
    pallas_call x1, Pallas kernels, on_device(): pl.pallas_call(block_kernel, out_shape=(jax.ShapeDtypeStruct((1024, 128),...  108 us

profile of v5, /device:TPU:27, one launch (start us, length us, event | category | flops | bytes accessed | tf_op | source)
XLA Modules:
  0.0 110.6 jit_solution(15182366119104640384)
XLA Ops:
  0.6 107.9 %shard_map.158 = (f32[1024,128]{1,0:T(8,128)}, f32[128,768]{1,0:T(8,128)}) custom-call(bf16[1024,128]{1,0:T(8,128)(2,1)} %bitcast.11, s32[32,32]{1,0:T(8,128)} %refs_1_.1, bf16[2,128,512]{2,1,0:T(8,128)(2,1)} %refs_2_.1, bf16[2,128,128]{2,1,0:T(8,128)(2,1)} %refs_3_.1, bf16[2,128,128]{2,1,0:T(8,128)(2,1)} %refs_4_.1, f32[2,2,128]{2,1,0:T(2,128)} %refs_5_.1, ...), custom_call_target="tpu_custom_call" | custom-call | flops 6000000000 | bytes 15000000 | tf_op jit(solution)/shard_map/pallas_call | solution.py:650
  108.6 2.0 %shard_map.159 = (f32[1024,128]{1,0:T(8,128)}, f32[128,768]{1,0:T(8,128)}) custom-call(f32[1024,128]{1,0:T(8,128)} %get-tuple-element.6.pair_ref, f32[128,768]{1,0:T(8,128)} %get-tuple-element.7.tokens_ref), custom_call_target="tpu_custom_call" | custom-call | tf_op jit(solution)/shard_map/pallas_call | solution.py:705

commit v6 on v5

--- a/solution.py
+++ b/solution.py
@@ -77,26 +77,15 @@
 
 
 class Burst:
-    def __init__(self, n, places, at, pair, device, src, dst, all_dst, most_src, send, recv):
-        self.n, self.places, self.at, self.pair = n, places, at, pair
-        self.device = device
+    def __init__(self, peers, me, src, dst, all_dst, most_src, send, recv):
+        self.peers, self.me = peers, me
         self.src, self.dst, self.all_dst, self.most_src = src, dst, all_dst, most_src
         self.send, self.recv = send, recv
 
     def start(self):
-        me, other = self.pair * self.n + self.at, 1 - self.pair
-        for place in self.places + [self.at]:
-            for pair in (other, self.pair):
-                if place is self.at and pair is self.pair:
-                    continue
-                remote(
-                    self.src(pair * self.n + place),
-                    self.dst(me),
-                    self.send,
-                    self.recv,
-                    self.device(pair, place),
-                ).start()
-        pltpu.make_async_copy(self.src(me), self.dst(me), self.recv).start()
+        for peer, device in self.peers:
+            remote(self.src(peer), self.dst(self.me), self.send, self.recv, device).start()
+        pltpu.make_async_copy(self.src(self.me), self.dst(self.me), self.recv).start()
 
     def wait(self):
         pltpu.make_async_copy(self.all_dst, self.all_dst, self.recv).wait()
@@ -182,27 +171,32 @@
     def on_col(peer):
         return {"col": peer}
 
-    def on_quad(pair, place):
-        return {"col": pair * 8 + place * 2 + core}
-
-    def on_rows(pair, place):
-        return {"group": pair, "row": place}
-
-    row_ring = ring(row, 8)
-    quad_at, quad_pair = lax.rem(quad, 4), lax.div(quad, 4)
-    quad_ring = ring(quad_at, 4)
+    quad_y = lax.rem(quad, 4)
+    chip_x = lax.div(quad, 4) * 2 + group
+    plane_me = group * 8 + quad
+    xs = [lax.rem(chip_x + d, 4) for d in range(4)]
+    ys = [lax.rem(quad_y + d, 4) for d in range(4)]
+    plane = []
+    far = ((2, 2), (2, 1), (2, 3), (1, 2), (3, 2), (1, 1), (3, 3), (1, 3), (3, 1))
+    for dx, dy in far + ((2, 0), (0, 2), (1, 0), (3, 0), (0, 1), (0, 3)):
+        high, low = lax.div(xs[dx], 2), lax.rem(xs[dx], 2)
+        place = high * 4 + ys[dy]
+        plane.append((low * 8 + place, {"group": low, "col": place * 2 + core}))
+    line = [(z, {"row": z}) for z in ring(row, 8)]
+    heads = [
+        (pair * 8 + place, on_col(pair * 8 + place))
+        for place in ring(lax.rem(col, 8), 8) + [lax.rem(col, 8)]
+        for pair in (1 - lax.div(col, 8), lax.div(col, 8))
+    ][:-1]
 
     barrier = pltpu.get_barrier_semaphore()
 
-    def greet(d):
-        place = lax.rem(big + d, 16)
-        for device in (
-            on_col(lax.rem(col + d, 16)),
-            on_rows(lax.div(place, 8), lax.rem(place, 8)),
-        ):
-            pl.semaphore_signal(barrier, inc=1, device_id=device, device_id_type=MESH)
-
-    loop(1, 16, greet)
+    def greet(device):
+        pl.semaphore_signal(barrier, inc=1, device_id=device, device_id_type=MESH)
+
+    loop(1, 16, lambda d: greet(on_col(lax.rem(col + d, 16))))
+    loop(1, 8, lambda d: greet({"row": lax.rem(row + d, 8)}))
+    loop(0, 8, lambda place: greet({"group": 1 - group, "col": place * 2 + core}))
 
     swap_s[...] = swap_matrix()
     pair_ref = held["pair"]
@@ -240,60 +234,48 @@
                 flat_s[pl.ds(two * 2 + t, 128, stride=8), :] = left
                 flat_s[pl.ds(4 + two * 2 + t, 128, stride=8), :] = right
             gate_s[pl.ds(it * 128, 256), :] = sigmoid(mm(zn, wg_ref[m]))
-        for s in range(8):
-            send_a[m, half, s] = flat_s[pl.ds(s * 128, 128), :].astype(BF16)
+        for block in range(16):
+            send_a[m, half, block] = flat_s[pl.ds(block * 64, 64), :].astype(BF16)
 
     def burst(stage, m, half):
         sems = ssem.at[stage * 4 + m * 2 + half], rsem.at[stage * 4 + m * 2 + half]
         if stage == 0:
             return Burst(
-                4,
-                quad_ring,
-                quad_at,
-                quad_pair,
-                on_quad,
+                plane,
+                plane_me,
                 lambda p: send_a.at[m, half, p],
                 lambda p: recv_a.at[m, half, p],
                 recv_a.at[m, half],
-                send_a.at[m, half, pl.ds(0, 7)],
+                send_a.at[m, half, pl.ds(0, 15)],
                 *sems,
             )
         if stage == 1:
             return Burst(
-                8,
-                row_ring,
+                line,
                 row,
-                group,
-                on_rows,
                 lambda p: send_b.at[m, half, p],
                 lambda p: recv_b.at[m, half, lax.div(p, 2), lax.rem(p, 2)],
                 recv_b.at[m, half],
-                send_b.at[m, half, pl.ds(0, 15)],
+                send_b.at[m, half, pl.ds(0, 7)],
                 *sems,
             )
         if stage == 2:
             return Burst(
-                8,
-                row_ring,
+                line,
                 row,
-                group,
-                on_rows,
                 lambda p: send_bt.at[m, half, p],
                 lambda p: recv_bt.at[m, half, p],
                 recv_bt.at[m, half],
-                send_bt.at[m, half, pl.ds(0, 15)],
+                send_bt.at[m, half, pl.ds(0, 7)],
                 *sems,
             )
         return Burst(
-            4,
-            quad_ring,
-            quad_at,
-            quad_pair,
-            on_quad,
+            plane,
+            plane_me,
             lambda p: send_at.at[m, half, p],
             lambda p: recv_at.at[m, half, p],
             recv_at.at[m, half],
-            send_at.at[m, half, pl.ds(0, 7)],
+            send_at.at[m, half, pl.ds(0, 15)],
             *sems,
         )
 
@@ -301,7 +283,7 @@
 
     def cross_left(m, half):
         return remote(
-            recv_b.at[m, half, :, :, 0],
+            recv_b.at[m, half, :, :, :, 0],
             x_left.at[m, half],
             cross_ssem.at[m * 2 + half],
             cross_rsem.at[m * 2 + half],
@@ -310,7 +292,7 @@
 
     def cross_right(half):
         return remote(
-            recv_b.at[0, half, :, 1 - core, 1],
+            recv_b.at[0, half, :, 1 - core, :, 1],
             x_right.at[half],
             cross_ssem.at[4 + half],
             cross_rsem.at[4 + half],
@@ -319,24 +301,38 @@
 
     def to_rows(m, half):
         for hi in range(2):
-            lanes = jnp.concatenate([recv_a[m, half, hi * 4 + lo] for lo in range(4)], axis=1)
+            lanes = jnp.concatenate(
+                [
+                    jnp.concatenate(
+                        [recv_a[m, half, pair * 8 + hi * 4 + lo] for lo in range(4)], axis=1
+                    )
+                    for pair in range(2)
+                ],
+                axis=0,
+            )
             moved = mm(lanes, swap_s[...])
             for lo in range(4):
                 mix_s[pl.ds(hi * 512 + lo, 128, stride=4), :] = moved[:, lo * 128 : (lo + 1) * 128]
         both = jnp.concatenate([mix_s[0:512, :], mix_s[512:1024, :]], axis=1)
-        send_b[m, half] = both.astype(BF16).reshape(16, 2, 16, 256)
+        both = both.astype(BF16).reshape(2, 8, 2, 16, 256)
+        for pair in range(2):
+            send_b[m, half, :, pair] = both[pair]
 
     def to_channels(m, half):
         for hi in range(2):
-            block = recv_bt[m, half, :, :, hi * 128 : (hi + 1) * 128]
-            mix_s[hi * 256 : (hi + 1) * 256, :] = block.astype(F32).reshape(256, 128)
+            for pair in range(2):
+                block = recv_bt[m, half, :, pair, :, hi * 128 : (hi + 1) * 128]
+                at = hi * 256 + pair * 128
+                mix_s[at : at + 128, :] = block.astype(F32).reshape(128, 128)
         for hi in range(2):
             lanes = jnp.concatenate(
                 [mix_s[pl.ds(hi * 256 + lo, 64, stride=4), :] for lo in range(4)], axis=1
             )
             moved = mm(lanes.astype(BF16), swap_s[...]).astype(BF16)
             for lo in range(4):
-                send_at[m, half, hi * 4 + lo] = moved[:, lo * 128 : (lo + 1) * 128]
+                part = moved[:, lo * 128 : (lo + 1) * 128]
+                for pair in range(2):
+                    send_at[m, half, pair * 8 + hi * 4 + lo] = part[pair * 32 : pair * 32 + 32]
 
     def triangle(m, gap):
         for half in range(2):
@@ -352,18 +348,25 @@
                 cross_left(m, half).start()
                 cross_right(half).start()
             right = jnp.concatenate(
-                [recv_b[m, half, s, core, 1] for s in range(8) for half in range(2)], axis=0
+                [
+                    recv_b[m, half, s % 4, core, s // 4, 1]
+                    for s in range(8)
+                    for half in range(2)
+                ],
+                axis=0,
             )
-            own = [mm(recv_b[m, half, :, :, 0].reshape(256, 256), right, NT) for half in range(2)]
+            own = [
+                mm(recv_b[m, half, :, :, :, 0].reshape(256, 256), right, NT) for half in range(2)
+            ]
             for half in range(2):
                 cross_left(m, half).wait_recv()
                 cross_right(half).wait_recv()
             right = jnp.concatenate(
-                [x_right[half, s] for s in range(8) for half in range(2)], axis=0
+                [x_right[half, s % 4, s // 4] for s in range(8) for half in range(2)], axis=0
             )
             for half in range(2):
                 total = own[half] + mm(x_left[m, half].reshape(256, 256), right, NT)
-                send_bt[m, half] = total.astype(BF16).reshape(16, 16, 256)
+                send_bt[m, half] = total.astype(BF16).reshape(8, 2, 16, 256)
                 burst(2, m, half).start()
             for half in range(2):
                 cross_right(half).wait_send()
@@ -372,8 +375,8 @@
             for half in range(2):
                 burst(1, m, half).wait()
                 cross_left(m, half).start()
-                right.append(recv_b[m, half, :, :, 1].reshape(256, 256))
-                term = mm(recv_b[m, half, :, :, 0].reshape(256, 256), right[half], TN)
+                right.append(recv_b[m, half, :, :, :, 1].reshape(256, 256))
+                term = mm(recv_b[m, half, :, :, :, 0].reshape(256, 256), right[half], TN)
                 own = term if half == 0 else own + term
             other = None
             for half in range(2):
@@ -383,8 +386,9 @@
             for half in range(2):
                 for s in range(8):
                     at = slice(s * 32 + half * 16, s * 32 + half * 16 + 16)
-                    send_bt[m, half, s * 2 + core] = own[at].astype(BF16)
-                    send_bt[m, half, s * 2 + 1 - core] = other[at].astype(BF16)
+                    z = s % 4 * 2
+                    send_bt[m, half, z + core, s // 4] = own[at].astype(BF16)
+                    send_bt[m, half, z + 1 - core, s // 4] = other[at].astype(BF16)
                 burst(2, m, half).start()
         for half in range(2):
             burst(1, m, half).drain()
@@ -462,11 +466,8 @@
             bias = mm(held["bw"][...], zn, NT).astype(BF16).astype(F32)
             heads_s[pl.ds(it, 16, stride=8), :] = bias
     to_head = Burst(
-        8,
-        ring(lax.rem(col, 8), 8),
-        lax.rem(col, 8),
-        lax.div(col, 8),
-        lambda pair, place: on_col(pair * 8 + place),
+        heads,
+        col,
         lambda p: heads_s.at[pl.ds(p * 8, 8)],
         lambda p: recv_h.at[p],
         recv_h,
@@ -666,16 +667,16 @@
             pltpu.VMEM((2, 128, 128), F32),
             pltpu.VMEM((8, 128), F32),
             pltpu.VMEM((512, 512), BF16),
-            pltpu.VMEM((2, 2, 8, 128, 128), BF16),
-            pltpu.VMEM((2, 2, 8, 128, 128), BF16),
-            pltpu.VMEM((2, 2, 16, 2, 16, 256), BF16),
+            pltpu.VMEM((2, 2, 16, 64, 128), BF16),
+            pltpu.VMEM((2, 2, 16, 64, 128), BF16),
             pltpu.VMEM((2, 2, 8, 2, 2, 16, 256), BF16),
+            pltpu.VMEM((2, 2, 4, 2, 2, 2, 16, 256), BF16),
+            pltpu.VMEM((2, 2, 4, 2, 2, 16, 256), BF16),
+            pltpu.VMEM((2, 4, 2, 16, 256), BF16),
             pltpu.VMEM((2, 2, 8, 2, 16, 256), BF16),
-            pltpu.VMEM((2, 8, 16, 256), BF16),
-            pltpu.VMEM((2, 2, 16, 16, 256), BF16),
-            pltpu.VMEM((2, 2, 16, 16, 256), BF16),
-            pltpu.VMEM((2, 2, 8, 64, 128), BF16),
-            pltpu.VMEM((2, 2, 8, 64, 128), BF16),
+            pltpu.VMEM((2, 2, 8, 2, 16, 256), BF16),
+            pltpu.VMEM((2, 2, 16, 32, 128), BF16),
+            pltpu.VMEM((2, 2, 16, 32, 128), BF16),
             pltpu.VMEM((128, 128), F32),
             pltpu.VMEM((16, 8, 128), F32),
             pltpu.VMEM((128, 128), F32),

time: 111 us -> 109 us (0.982)
  Pallas kernels: 110 us -> 108 us
    pallas_call x1, Pallas kernels: 108 us -> 106 us  [on_device(): pl.pallas_call(block_kernel, out_shape=(jax.ShapeDtypeStruct((1024, 128),...]
where the time goes in v6:
time: 109 us; the launch traced here: 108 us
  Pallas kernels  108 us (99%)
    pallas_call x1, Pallas kernels, on_device(): pl.pallas_call(block_kernel, out_shape=(jax.ShapeDtypeStruct((1024, 128),...  106 us

profile of v6, /device:TPU:27, one launch (start us, length us, event | category | flops | bytes accessed | tf_op | source)
XLA Modules:
  0.0 108.4 jit_solution(15800314839952953708)
XLA Ops:
  0.6 105.7 %shard_map.158 = (f32[1024,128]{1,0:T(8,128)}, f32[128,768]{1,0:T(8,128)}) custom-call(bf16[1024,128]{1,0:T(8,128)(2,1)} %bitcast.11, s32[32,32]{1,0:T(8,128)} %refs_1_.1, bf16[2,128,512]{2,1,0:T(8,128)(2,1)} %refs_2_.1, bf16[2,128,128]{2,1,0:T(8,128)(2,1)} %refs_3_.1, bf16[2,128,128]{2,1,0:T(8,128)(2,1)} %refs_4_.1, f32[2,2,128]{2,1,0:T(2,128)} %refs_5_.1, ...), custom_call_target="tpu_custom_call" | custom-call | flops 6000000000 | bytes 15000000 | tf_op jit(solution)/shard_map/pallas_call | solution.py:651
  106.4 2.0 %shard_map.159 = (f32[1024,128]{1,0:T(8,128)}, f32[128,768]{1,0:T(8,128)}) custom-call(f32[1024,128]{1,0:T(8,128)} %get-tuple-element.6.pair_ref, f32[128,768]{1,0:T(8,128)} %get-tuple-element.7.tokens_ref), custom_call_target="tpu_custom_call" | custom-call | tf_op jit(solution)/shard_map/pallas_call | solution.py:706

commit v7 on v6

--- a/solution.py
+++ b/solution.py
@@ -165,7 +165,9 @@
         name: pltpu.make_async_copy(inputs[name], held[name], load_sem.at[i])
         for i, name in enumerate(NAMES)
     }
-    for name in NAMES:
+    early = ("pair", "wp", "mask", "gains", "wg")
+    late = ("wo", "bgain", "bw", "tokens", "again", "watt", "wout", "tgain", "wup", "wdown")
+    for name in early:
         loads[name].start()
 
     def on_col(peer):
@@ -202,12 +204,12 @@
     pair_ref = held["pair"]
     wg_ref, wo_ref = held["wg"], held["wo"]
 
-    for name in ("pair", "mask", "wp", "wg", "wo", "gains", "bgain", "bw"):
+    for name in early:
         loads[name].wait()
+    for name in late:
+        loads[name].start()
     gain_in = [held["gains"][m, 0:1, :] for m in range(2)]
-    for m in range(2):
-        wpt_s[m] = held["wp"][m].T
-        gmid_s[m] = jnp.broadcast_to(held["gains"][m, 1:2, :], (128, 128)).T
+    wpt_s[0] = held["wp"][0].T
     mask = held["mask"][...].astype(F32).astype(BF16)
     picked = []
     for lo in range(4):
@@ -438,7 +440,11 @@
             scores_s[s] = mm(qkv_s[s, 0:48, :], qkv_s[s, 48:96, :], TN) * (48.0**-0.5)
 
     def gap_first():
-        for name in ("tokens", "again", "watt"):
+        wpt_s[1] = held["wp"][1].T
+        for m in range(2):
+            gmid_s[m] = jnp.broadcast_to(held["gains"][m, 1:2, :], (128, 128)).T
+        heads_s[...] = jnp.zeros_like(heads_s)
+        for name in ("wo", "bgain", "bw", "tokens", "again", "watt"):
             loads[name].wait()
         project((0, 1))
 
@@ -455,6 +461,19 @@
         burst(0, 1, half).start()
     for half in range(2):
         burst(3, 0, half).drain()
+
+    def to_head(half):
+        return Burst(
+            heads,
+            col,
+            lambda p: heads_s.at[half, pl.ds(p * 8, 8)],
+            lambda p: recv_h.at[half, p],
+            recv_h.at[half],
+            heads_s.at[half, pl.ds(0, 120)],
+            ssem.at[16 + half],
+            rsem.at[16 + half],
+        )
+
     triangle(1, lambda: project((2, 3)))
     for half in range(2):
         burst(3, 1, half).wait()
@@ -464,66 +483,61 @@
             out_ref[pl.ds(it * 128, 128), :] = z
             zn = normalize(z, held["bgain"][...]).astype(BF16)
             bias = mm(held["bw"][...], zn, NT).astype(BF16).astype(F32)
-            heads_s[pl.ds(it, 16, stride=8), :] = bias
-    to_head = Burst(
-        heads,
-        col,
-        lambda p: heads_s.at[pl.ds(p * 8, 8)],
-        lambda p: recv_h.at[p],
-        recv_h,
-        heads_s.at[pl.ds(0, 120)],
-        ssem.at[16],
-        rsem.at[16],
-    )
-    to_head.start()
+            heads_s[half, pl.ds(it % 4, 16, stride=8), :] = bias
+        to_head(half).start()
+
+    def along(half, offset):
+        block = bias_s.at[big, pl.ds(half * 16, 16)]
+        return remote(
+            block,
+            block,
+            many_ssem.at[half, offset],
+            many_rsem.at[half, offset],
+            {"row": lax.rem(row + offset, 8)},
+        )
+
+    def across(half, owner, z):
+        block = bias_s.at[owner * 8 + z, pl.ds(half * 16, 16)]
+        return remote(
+            block,
+            block,
+            many_ssem.at[half, 8 + z],
+            many_rsem.at[half, 8 + z],
+            {"group": 1 - group},
+        )
+
+    for half in range(2):
+        to_head(half).wait()
+        lanes = jnp.concatenate(
+            [
+                jnp.concatenate([recv_h[half, hi * 4 + lo] for lo in range(4)], axis=1)
+                for hi in range(4)
+            ],
+            axis=0,
+        ).astype(BF16)
+        moved = mm(lanes, swap_s[...])
+        for hi in range(4):
+            for lo in range(4):
+                rows_s[pl.ds(hi * 32 + lo, 8, stride=4), :] = moved[
+                    hi * 8 : (hi + 1) * 8, lo * 128 : (lo + 1) * 128
+                ]
+        bias_s[big, half * 16 : (half + 1) * 16, :] = jnp.concatenate(
+            [rows_s[hi * 32 : hi * 32 + 16, :] for hi in range(4)], axis=1
+        ).astype(BF16)
+        for offset in (4, 3, 5, 2, 6, 1, 7):
+            along(half, offset).start()
+        across(half, group, row).start()
     for half in range(2):
         burst(3, 1, half).drain()
-    to_head.wait()
-    lanes = jnp.concatenate(
-        [
-            jnp.concatenate([recv_h[hi * 4 + lo] for lo in range(4)], axis=1)
-            for hi in range(4)
-        ],
-        axis=0,
-    ).astype(BF16)
-    moved = mm(lanes, swap_s[...])
-    for hi in range(4):
-        for lo in range(4):
-            rows_s[pl.ds(hi * 32 + lo, 8, stride=4), :] = moved[
-                hi * 8 : (hi + 1) * 8, lo * 128 : (lo + 1) * 128
-            ]
-    bias_s[big] = jnp.concatenate(
-        [rows_s[hi * 32 : (hi + 1) * 32, :] for hi in range(4)], axis=1
-    ).astype(BF16)
-    def along(offset):
-        return remote(
-            bias_s.at[big],
-            bias_s.at[big],
-            many_ssem.at[0, offset],
-            many_rsem.at[0, offset],
-            {"row": lax.rem(row + offset, 8)},
-        )
-
-    def across(owner, z):
-        return remote(
-            bias_s.at[owner * 8 + z],
-            bias_s.at[owner * 8 + z],
-            many_ssem.at[0, 8 + z],
-            many_rsem.at[0, 8 + z],
-            {"group": 1 - group},
-        )
-
-    across(group, row).start()
-    for offset in (4, 3, 5, 2, 6, 1, 7):
-        along(offset).start()
+
     to_tokens = Exchange(
         16,
         col,
         on_col,
         lambda p: send_o.at[p],
         lambda p: recv_o.at[p],
-        many_ssem.at[1],
-        many_rsem.at[1],
+        many_ssem.at[2],
+        many_rsem.at[2],
     )
 
     def attend(step, carry):
@@ -535,12 +549,14 @@
 
             @pl.when(jnp.logical_and(step < 2, z != row))
             def _():
-                along(lax.rem(row - z + 8, 8)).wait_recv()
-                across(owner, z).start()
+                for half in range(2):
+                    along(half, lax.rem(row - z + 8, 8)).wait_recv()
+                    across(half, owner, z).start()
 
             @pl.when(step >= 2)
             def _():
-                across(owner, z).wait_recv()
+                for half in range(2):
+                    across(half, owner, z).wait_recv()
 
         bias = bias_s[pl.ds(part * 4, 4)].reshape(128, 512).astype(F32)
         rows = pl.ds(pl.multiple_of(part * 128, 128), 128)
@@ -568,9 +584,10 @@
 
     lax.fori_loop(0, 4, attend, 0)
 
-    loop(1, 8, lambda d: along(d).wait_send())
-    loop(0, 8, lambda z: across(group, z).wait_send())
-    to_head.drain()
+    for half in range(2):
+        loop(1, 8, lambda d: along(half, d).wait_send())
+        loop(0, 8, lambda z: across(half, group, z).wait_send())
+        to_head(half).drain()
     for name in ("wout", "tgain", "wup", "wdown"):
         loads[name].wait()
     own = [
@@ -677,8 +694,8 @@
             pltpu.VMEM((2, 2, 8, 2, 16, 256), BF16),
             pltpu.VMEM((2, 2, 16, 32, 128), BF16),
             pltpu.VMEM((2, 2, 16, 32, 128), BF16),
-            pltpu.VMEM((128, 128), F32),
-            pltpu.VMEM((16, 8, 128), F32),
+            pltpu.VMEM((2, 128, 128), F32),
+            pltpu.VMEM((2, 16, 8, 128), F32),
             pltpu.VMEM((128, 128), F32),
             pltpu.VMEM((16, 32, 512), BF16),
             pltpu.VMEM((512, 768), BF16),
@@ -688,12 +705,12 @@
             pltpu.VMEM((48, 512), BF16),
             pltpu.VMEM((16, 48, 128), BF16),
             pltpu.VMEM((16, 48, 128), BF16),
-            pltpu.SemaphoreType.DMA((17,)),
-            pltpu.SemaphoreType.DMA((17,)),
+            pltpu.SemaphoreType.DMA((18,)),
+            pltpu.SemaphoreType.DMA((18,)),
             pltpu.SemaphoreType.DMA((6,)),
             pltpu.SemaphoreType.DMA((6,)),
-            pltpu.SemaphoreType.DMA((2, 16)),
-            pltpu.SemaphoreType.DMA((2, 16)),
+            pltpu.SemaphoreType.DMA((3, 16)),
+            pltpu.SemaphoreType.DMA((3, 16)),
             pltpu.SemaphoreType.DMA((15,)),
         ],
         compiler_params=pltpu.CompilerParams(

time: 109 us -> 107 us (0.982)
  Pallas kernels: 108 us -> 106 us
    pallas_call x1, Pallas kernels: 106 us -> 104 us  [on_device(): pl.pallas_call(block_kernel, out_shape=(jax.ShapeDtypeStruct((1024, 128),...]
where the time goes in v7:
time: 107 us
  Pallas kernels  106 us (99%)
    pallas_call x1, Pallas kernels, on_device(): pl.pallas_call(block_kernel, out_shape=(jax.ShapeDtypeStruct((1024, 128),...  104 us

profile of v7, /device:TPU:27, one launch (start us, length us, event | category | flops | bytes accessed | tf_op | source)
XLA Modules:
  0.0 106.7 jit_solution(13628566254718688039)
XLA Ops:
  0.6 104.0 %shard_map.158 = (f32[1024,128]{1,0:T(8,128)}, f32[128,768]{1,0:T(8,128)}) custom-call(bf16[1024,128]{1,0:T(8,128)(2,1)} %bitcast.11, s32[32,32]{1,0:T(8,128)} %refs_1_.1, bf16[2,128,512]{2,1,0:T(8,128)(2,1)} %refs_2_.1, bf16[2,128,128]{2,1,0:T(8,128)(2,1)} %refs_3_.1, bf16[2,128,128]{2,1,0:T(8,128)(2,1)} %refs_4_.1, f32[2,2,128]{2,1,0:T(2,128)} %refs_5_.1, ...), custom_call_target="tpu_custom_call" | custom-call | flops 6000000000 | bytes 15000000 | tf_op jit(solution)/shard_map/pallas_call | solution.py:668
  104.6 2.0 %shard_map.159 = (f32[1024,128]{1,0:T(8,128)}, f32[128,768]{1,0:T(8,128)}) custom-call(f32[1024,128]{1,0:T(8,128)} %get-tuple-element.6.pair_ref, f32[128,768]{1,0:T(8,128)} %get-tuple-element.7.tokens_ref), custom_call_target="tpu_custom_call" | custom-call | tf_op jit(solution)/shard_map/pallas_call | solution.py:723

commit v8 on v7

--- a/solution.py
+++ b/solution.py
@@ -127,6 +127,8 @@
         gmid_s,
         mask_s,
         swap_s,
+        send_z,
+        recv_z,
         send_a,
         recv_a,
         send_b,
@@ -236,8 +238,13 @@
                 flat_s[pl.ds(two * 2 + t, 128, stride=8), :] = left
                 flat_s[pl.ds(4 + two * 2 + t, 128, stride=8), :] = right
             gate_s[pl.ds(it * 128, 256), :] = sigmoid(mm(zn, wg_ref[m]))
-        for block in range(16):
-            send_a[m, half, block] = flat_s[pl.ds(block * 64, 64), :].astype(BF16)
+        if half == 0:
+            for z in range(8):
+                rows = [flat_s[pl.ds(block * 64 + z * 8, 8), :] for block in range(16)]
+                send_z[m, z] = jnp.concatenate(rows, axis=0).astype(BF16)
+        else:
+            for block in range(16):
+                send_a[m, half, block] = flat_s[pl.ds(block * 64, 64), :].astype(BF16)
 
     def burst(stage, m, half):
         sems = ssem.at[stage * 4 + m * 2 + half], rsem.at[stage * 4 + m * 2 + half]
@@ -251,14 +258,24 @@
                 send_a.at[m, half, pl.ds(0, 15)],
                 *sems,
             )
+        if stage == 1 and half == 0:
+            return Burst(
+                line,
+                row,
+                lambda p: send_z.at[m, p],
+                lambda p: recv_z.at[m, p],
+                recv_z.at[m],
+                send_z.at[m, pl.ds(0, 7)],
+                *sems,
+            )
         if stage == 1:
             return Burst(
                 line,
                 row,
-                lambda p: send_b.at[m, half, p],
+                lambda p: send_b.at[m, p],
                 lambda p: recv_b.at[m, half, lax.div(p, 2), lax.rem(p, 2)],
                 recv_b.at[m, half],
-                send_b.at[m, half, pl.ds(0, 7)],
+                send_b.at[m, pl.ds(0, 7)],
                 *sems,
             )
         if stage == 2:
@@ -301,6 +318,12 @@
             partner,
         )
 
+    def regroup(m):
+        held_z = [recv_z[m, z].astype(F32) for z in range(8)]
+        for block in range(16):
+            rows = [held_z[z][block * 8 : (block + 1) * 8] for z in range(8)]
+            send_a[m, 0, block] = jnp.concatenate(rows, axis=0).astype(BF16)
+
     def to_rows(m, half):
         for hi in range(2):
             lanes = jnp.concatenate(
@@ -318,7 +341,10 @@
         both = jnp.concatenate([mix_s[0:512, :], mix_s[512:1024, :]], axis=1)
         both = both.astype(BF16).reshape(2, 8, 2, 16, 256)
         for pair in range(2):
-            send_b[m, half, :, pair] = both[pair]
+            if half == 0:
+                recv_b[m, half, :, :, pair] = both[pair].reshape(4, 2, 2, 16, 256)
+            else:
+                send_b[m, :, pair] = both[pair]
 
     def to_channels(m, half):
         for hi in range(2):
@@ -337,16 +363,25 @@
                     send_at[m, half, pair * 8 + hi * 4 + lo] = part[pair * 32 : pair * 32 + 32]
 
     def triangle(m, gap):
-        for half in range(2):
-            burst(0, m, half).wait()
-            to_rows(m, half)
-            burst(1, m, half).start()
+        burst(0, m, 1).wait()
+        to_rows(m, 1)
+        burst(1, m, 1).start()
+        burst(1, m, 0).wait()
+        regroup(m)
+        burst(0, m, 0).start()
         gap()
-        for half in range(2):
-            burst(0, m, half).drain()
+        burst(0, m, 1).drain()
+
+        def arrive(half):
+            if half == 0:
+                burst(0, m, 0).wait()
+                to_rows(m, 0)
+            else:
+                burst(1, m, 1).wait()
+
         if m == 0:
             for half in range(2):
-                burst(1, m, half).wait()
+                arrive(half)
                 cross_left(m, half).start()
                 cross_right(half).start()
             right = jnp.concatenate(
@@ -375,7 +410,7 @@
         else:
             right, own = [], None
             for half in range(2):
-                burst(1, m, half).wait()
+                arrive(half)
                 cross_left(m, half).start()
                 right.append(recv_b[m, half, :, :, :, 1].reshape(256, 256))
                 term = mm(recv_b[m, half, :, :, :, 0].reshape(256, 256), right[half], TN)
@@ -392,6 +427,7 @@
                     send_bt[m, half, z + core, s // 4] = own[at].astype(BF16)
                     send_bt[m, half, z + 1 - core, s // 4] = other[at].astype(BF16)
                 burst(2, m, half).start()
+        burst(0, m, 0).drain()
         for half in range(2):
             burst(1, m, half).drain()
             cross_left(m, half).wait_send()
@@ -450,7 +486,7 @@
 
     edges(0, 0, first_state)
     pl.semaphore_wait(barrier, 30)
-    burst(0, 0, 0).start()
+    burst(1, 0, 0).start()
     edges(0, 1, first_state)
     burst(0, 0, 1).start()
     triangle(0, gap_first)
@@ -458,7 +494,7 @@
         burst(3, 0, half).wait()
         middle_norm(0, half)
         edges(1, half, second_state)
-        burst(0, 1, half).start()
+        burst(1 - half, 1, half).start()
     for half in range(2):
         burst(3, 0, half).drain()
 
@@ -684,9 +720,11 @@
             pltpu.VMEM((2, 128, 128), F32),
             pltpu.VMEM((8, 128), F32),
             pltpu.VMEM((512, 512), BF16),
+            pltpu.VMEM((2, 8, 128, 128), BF16),
+            pltpu.VMEM((2, 8, 128, 128), BF16),
             pltpu.VMEM((2, 2, 16, 64, 128), BF16),
             pltpu.VMEM((2, 2, 16, 64, 128), BF16),
-            pltpu.VMEM((2, 2, 8, 2, 2, 16, 256), BF16),
+            pltpu.VMEM((2, 8, 2, 2, 16, 256), BF16),
             pltpu.VMEM((2, 2, 4, 2, 2, 2, 16, 256), BF16),
             pltpu.VMEM((2, 2, 4, 2, 2, 16, 256), BF16),
             pltpu.VMEM((2, 4, 2, 16, 256), BF16),

time: 107 us -> 97.3 us (0.909)
  Pallas kernels: 106 us -> 96.5 us
    pallas_call x1, Pallas kernels: 104 us -> 94.5 us  [on_device(): pl.pallas_call(block_kernel, out_shape=(jax.ShapeDtypeStruct((1024, 128),...]
where the time goes in v8:
time: 97.3 us; the launch traced here: 97.1 us
  Pallas kernels  96.5 us (99%)
    pallas_call x1, Pallas kernels, on_device(): pl.pallas_call(block_kernel, out_shape=(jax.ShapeDtypeStruct((1024, 128),...  94.5 us
    pallas_call x1, Pallas kernels, on_device(): pl.pallas_call(close_kernel, out_shape=(jax.ShapeDtypeStruct((1024, 128),...  2.05 us

profile of v8, /device:TPU:27, one launch (start us, length us, event | category | flops | bytes accessed | tf_op | source)
XLA Modules:
  0.0 97.1 jit_solution(12992131704730641646)
XLA Ops:
  0.6 94.5 %shard_map.158 = (f32[1024,128]{1,0:T(8,128)}, f32[128,768]{1,0:T(8,128)}) custom-call(bf16[1024,128]{1,0:T(8,128)(2,1)} %bitcast.11, s32[32,32]{1,0:T(8,128)} %refs_1_.1, bf16[2,128,512]{2,1,0:T(8,128)(2,1)} %refs_2_.1, bf16[2,128,128]{2,1,0:T(8,128)(2,1)} %refs_3_.1, bf16[2,128,128]{2,1,0:T(8,128)(2,1)} %refs_4_.1, f32[2,2,128]{2,1,0:T(2,128)} %refs_5_.1, ...), custom_call_target="tpu_custom_call" | custom-call | flops 6000000000 | bytes 15000000 | tf_op jit(solution)/shard_map/pallas_call | solution.py:704
  95.1 2.0 %shard_map.159 = (f32[1024,128]{1,0:T(8,128)}, f32[128,768]{1,0:T(8,128)}) custom-call(f32[1024,128]{1,0:T(8,128)} %get-tuple-element.6.pair_ref, f32[128,768]{1,0:T(8,128)} %get-tuple-element.7.tokens_ref), custom_call_target="tpu_custom_call" | custom-call | tf_op jit(solution)/shard_map/pallas_call | solution.py:761

commit v9 on v8

--- a/solution.py
+++ b/solution.py
@@ -125,6 +125,7 @@
         mix_s,
         wpt_s,
         gmid_s,
+        wout_s,
         mask_s,
         swap_s,
         send_z,
@@ -135,6 +136,8 @@
         recv_b,
         x_left,
         x_right,
+        send_zt,
+        recv_zt,
         send_bt,
         recv_bt,
         send_at,
@@ -278,13 +281,23 @@
                 send_b.at[m, pl.ds(0, 7)],
                 *sems,
             )
+        if stage == 2 and half == 1:
+            return Burst(
+                line,
+                row,
+                lambda p: send_zt.at[m, p],
+                lambda p: recv_zt.at[m, p],
+                recv_zt.at[m],
+                send_zt.at[m, pl.ds(0, 7)],
+                *sems,
+            )
         if stage == 2:
             return Burst(
                 line,
                 row,
                 lambda p: send_bt.at[m, half, p],
-                lambda p: recv_bt.at[m, half, p],
-                recv_bt.at[m, half],
+                lambda p: recv_bt.at[m, p],
+                recv_bt.at[m],
                 send_bt.at[m, half, pl.ds(0, 7)],
                 *sems,
             )
@@ -349,7 +362,10 @@
     def to_channels(m, half):
         for hi in range(2):
             for pair in range(2):
-                block = recv_bt[m, half, :, pair, :, hi * 128 : (hi + 1) * 128]
+                if half == 0:
+                    block = recv_bt[m, :, pair, :, hi * 128 : (hi + 1) * 128]
+                else:
+                    block = send_bt[m, half, :, pair, :, hi * 128 : (hi + 1) * 128]
                 at = hi * 256 + pair * 128
                 mix_s[at : at + 128, :] = block.astype(F32).reshape(128, 128)
         for hi in range(2):
@@ -361,6 +377,15 @@
                 part = moved[:, lo * 128 : (lo + 1) * 128]
                 for pair in range(2):
                     send_at[m, half, pair * 8 + hi * 4 + lo] = part[pair * 32 : pair * 32 + 32]
+
+    def regroup_back(m):
+        mix_s[0:512, :] = recv_at[m, 1].astype(F32).reshape(512, 128)
+        for z in range(8):
+            for t in range(4):
+                mix_s[pl.ds(512 + z * 64 + t, 16, stride=4), :] = mix_s[
+                    pl.ds(z * 4 + t, 16, stride=32), :
+                ]
+            send_zt[m, z] = mix_s[pl.ds(512 + z * 64, 64), :].astype(BF16)
 
     def triangle(m, gap):
         burst(0, m, 1).wait()
@@ -378,6 +403,13 @@
                 to_rows(m, 0)
             else:
                 burst(1, m, 1).wait()
+
+        def send_back(half):
+            if half == 0:
+                burst(2, m, 0).start()
+            else:
+                to_channels(m, 1)
+                burst(3, m, 1).start()
 
         if m == 0:
             for half in range(2):
@@ -404,7 +436,7 @@
             for half in range(2):
                 total = own[half] + mm(x_left[m, half].reshape(256, 256), right, NT)
                 send_bt[m, half] = total.astype(BF16).reshape(8, 2, 16, 256)
-                burst(2, m, half).start()
+                send_back(half)
             for half in range(2):
                 cross_right(half).wait_send()
         else:
@@ -426,20 +458,28 @@
                     z = s % 4 * 2
                     send_bt[m, half, z + core, s // 4] = own[at].astype(BF16)
                     send_bt[m, half, z + 1 - core, s // 4] = other[at].astype(BF16)
-                burst(2, m, half).start()
+                send_back(half)
         burst(0, m, 0).drain()
         for half in range(2):
             burst(1, m, half).drain()
             cross_left(m, half).wait_send()
-        for half in range(2):
-            burst(2, m, half).wait()
-            to_channels(m, half)
-            burst(3, m, half).start()
-        for half in range(2):
-            burst(2, m, half).drain()
+        burst(3, m, 1).wait()
+        regroup_back(m)
+        burst(2, m, 1).start()
+        burst(2, m, 0).wait()
+        to_channels(m, 0)
+        burst(3, m, 0).start()
+        burst(2, m, 0).drain()
+        burst(3, m, 1).drain()
 
     def middle_norm(m, half):
-        summed = recv_at[m, half].astype(F32).reshape(64, 8, 128)
+        if half == 0:
+            burst(3, m, 0).wait()
+            summed = recv_at[m, 0]
+        else:
+            burst(2, m, 1).wait()
+            summed = recv_zt[m]
+        summed = summed.astype(F32).reshape(64, 8, 128)
 
         def over_channels(value):
             pairs = jnp.sum(value, axis=0)
@@ -450,8 +490,9 @@
         nrm_s[...] = (mean_removed * lax.rsqrt(variance + EPS)[None]).reshape(512, 128)
 
     def update(m, it):
-        normed = (nrm_s[pl.ds(it % 4, 128, stride=4), :] * gmid_s[m]).astype(BF16)
-        return gate_s[pl.ds(it * 128, 128), :] * mm(normed, wo_ref[m], TN)
+        half = it // 4
+        normed = (nrm_s[pl.ds(it % 4, 128, stride=4), :] * gmid_s[half * 2 + m]).astype(BF16)
+        return gate_s[pl.ds(it * 128, 128), :] * mm(normed, wout_s[half * 2 + m], TN)
 
     def first_state(it):
         return pair_ref[pl.ds(it * 128, 128), :].astype(F32)
@@ -477,11 +518,18 @@
 
     def gap_first():
         wpt_s[1] = held["wp"][1].T
-        for m in range(2):
-            gmid_s[m] = jnp.broadcast_to(held["gains"][m, 1:2, :], (128, 128)).T
         heads_s[...] = jnp.zeros_like(heads_s)
         for name in ("wo", "bgain", "bw", "tokens", "again", "watt"):
             loads[name].wait()
+        for m in range(2):
+            gmid_s[m] = jnp.broadcast_to(held["gains"][m, 1:2, :], (128, 128)).T
+            wout_s[m] = wo_ref[m]
+            mix_s[0:128, :] = gmid_s[m]
+            mix_s[128:256, :] = wo_ref[m].astype(F32)
+            for z in range(8):
+                rows = slice(z * 16, z * 16 + 16)
+                gmid_s[2 + m, rows, :] = mix_s[pl.ds(z, 16, stride=8), :]
+                wout_s[2 + m, rows, :] = mix_s[pl.ds(128 + z, 16, stride=8), :].astype(BF16)
         project((0, 1))
 
     edges(0, 0, first_state)
@@ -491,12 +539,11 @@
     burst(0, 0, 1).start()
     triangle(0, gap_first)
     for half in range(2):
-        burst(3, 0, half).wait()
         middle_norm(0, half)
         edges(1, half, second_state)
         burst(1 - half, 1, half).start()
-    for half in range(2):
-        burst(3, 0, half).drain()
+    burst(3, 0, 0).drain()
+    burst(2, 0, 1).drain()
 
     def to_head(half):
         return Burst(
@@ -512,7 +559,6 @@
 
     triangle(1, lambda: project((2, 3)))
     for half in range(2):
-        burst(3, 1, half).wait()
         middle_norm(1, half)
         for it in range(half * 4, half * 4 + 4):
             z = z_s[pl.ds(it * 128, 128), :] + update(1, it)
@@ -563,8 +609,8 @@
         for offset in (4, 3, 5, 2, 6, 1, 7):
             along(half, offset).start()
         across(half, group, row).start()
-    for half in range(2):
-        burst(3, 1, half).drain()
+    burst(3, 1, 0).drain()
+    burst(2, 1, 1).drain()
 
     to_tokens = Exchange(
         16,
@@ -717,7 +763,8 @@
             pltpu.VMEM((512, 128), F32),
             pltpu.VMEM((1024, 128), F32),
             pltpu.VMEM((2, 512, 128), BF16),
-            pltpu.VMEM((2, 128, 128), F32),
+            pltpu.VMEM((4, 128, 128), F32),
+            pltpu.VMEM((4, 128, 128), BF16),
             pltpu.VMEM((8, 128), F32),
             pltpu.VMEM((512, 512), BF16),
             pltpu.VMEM((2, 8, 128, 128), BF16),
@@ -728,8 +775,10 @@
             pltpu.VMEM((2, 2, 4, 2, 2, 2, 16, 256), BF16),
             pltpu.VMEM((2, 2, 4, 2, 2, 16, 256), BF16),
             pltpu.VMEM((2, 4, 2, 16, 256), BF16),
+            pltpu.VMEM((2, 8, 64, 128), BF16),
+            pltpu.VMEM((2, 8, 64, 128), BF16),
             pltpu.VMEM((2, 2, 8, 2, 16, 256), BF16),
-            pltpu.VMEM((2, 2, 8, 2, 16, 256), BF16),
+            pltpu.VMEM((2, 8, 2, 16, 256), BF16),
             pltpu.VMEM((2, 2, 16, 32, 128), BF16),
             pltpu.VMEM((2, 2, 16, 32, 128), BF16),
             pltpu.VMEM((2, 128, 128), F32),

time: 97.3 us -> 95.5 us (0.982)
  Pallas kernels: 96.5 us -> 94.7 us
    pallas_call x1, Pallas kernels: 94.5 us -> 92.7 us  [on_device(): pl.pallas_call(block_kernel, out_shape=(jax.ShapeDtypeStruct((1024, 128),...]
where the time goes in v9:
time: 95.5 us; the launch traced here: 95.4 us
  Pallas kernels  94.7 us (99%)
    pallas_call x1, Pallas kernels, on_device(): pl.pallas_call(block_kernel, out_shape=(jax.ShapeDtypeStruct((1024, 128),...  92.7 us
    pallas_call x1, Pallas kernels, on_device(): pl.pallas_call(close_kernel, out_shape=(jax.ShapeDtypeStruct((1024, 128),...  2.05 us

profile of v9, /device:TPU:27, one launch (start us, length us, event | category | flops | bytes accessed | tf_op | source)
XLA Modules:
  0.0 95.4 jit_solution(4350553359964672714)
XLA Ops:
  0.6 92.7 %shard_map.158 = (f32[1024,128]{1,0:T(8,128)}, f32[128,768]{1,0:T(8,128)}) custom-call(bf16[1024,128]{1,0:T(8,128)(2,1)} %bitcast.11, s32[32,32]{1,0:T(8,128)} %refs_1_.1, bf16[2,128,512]{2,1,0:T(8,128)(2,1)} %refs_2_.1, bf16[2,128,128]{2,1,0:T(8,128)(2,1)} %refs_3_.1, bf16[2,128,128]{2,1,0:T(8,128)(2,1)} %refs_4_.1, f32[2,2,128]{2,1,0:T(2,128)} %refs_5_.1, ...), custom_call_target="tpu_custom_call" | custom-call | flops 6000000000 | bytes 15000000 | tf_op jit(solution)/shard_map/pallas_call | solution.py:750
  93.3 2.0 %shard_map.159 = (f32[1024,128]{1,0:T(8,128)}, f32[128,768]{1,0:T(8,128)}) custom-call(f32[1024,128]{1,0:T(8,128)} %get-tuple-element.6.pair_ref, f32[128,768]{1,0:T(8,128)} %get-tuple-element.7.tokens_ref), custom_call_target="tpu_custom_call" | custom-call | tf_op jit(solution)/shard_map/pallas_call | solution.py:810

commit v10 on v9

--- a/solution.py
+++ b/solution.py
@@ -77,21 +77,38 @@
 
 
 class Burst:
-    def __init__(self, peers, me, src, dst, all_dst, most_src, send, recv):
-        self.peers, self.me = peers, me
+    def __init__(self, peers, me, src, dst, all_dst, most_src, send, recv, relay=None):
+        self.peers, self.me, self.relay = peers, me, relay
         self.src, self.dst, self.all_dst, self.most_src = src, dst, all_dst, most_src
         self.send, self.recv = send, recv
 
     def start(self):
-        for peer, device in self.peers:
+        peers = self.peers
+        if self.relay is not None:
+            part, held, arrived, _, _, target = self.relay
+            peer, device = peers[0]
+            remote(part(self.src(peer), 1), held, self.send, arrived, target).start()
+            remote(
+                part(self.src(peer), 0), part(self.dst(self.me), 0), self.send, self.recv, device
+            ).start()
+            peers = peers[1:]
+        for peer, device in peers:
             remote(self.src(peer), self.dst(self.me), self.send, self.recv, device).start()
         pltpu.make_async_copy(self.src(self.me), self.dst(self.me), self.recv).start()
 
     def wait(self):
         pltpu.make_async_copy(self.all_dst, self.all_dst, self.recv).wait()
 
+    def forward(self):
+        part, held, arrived, left, source, target = self.relay
+        pltpu.make_async_copy(held, held, arrived).wait()
+        remote(held, part(self.dst(source), 1), left, self.recv, target).start()
+
     def drain(self):
         pltpu.make_async_copy(self.most_src, self.most_src, self.send).wait()
+        if self.relay is not None:
+            _, held, _, left, _, _ = self.relay
+            pltpu.make_async_copy(held, held, left).wait()
 
 
 NAMES = (
@@ -160,6 +177,12 @@
         many_ssem,
         many_rsem,
         load_sem,
+        relay_1,
+        relay_2,
+        relay_3,
+        relay_4,
+        relay_ssem,
+        relay_rsem,
     ) = refs[32:]
     group, row, col = (lax.axis_index(name) for name in ("group", "row", "col"))
     big = group * 8 + row
@@ -249,6 +272,22 @@
             for block in range(16):
                 send_a[m, half, block] = flat_s[pl.ds(block * 64, 64), :].astype(BF16)
 
+    def relay(stage, m, half):
+        at = (stage - 1) * 4 + m * 2 + half
+        held = ((relay_1, relay_2), (relay_3, relay_4))[stage - 1][half].at[m]
+        if half == stage - 1:
+            size = 64 if stage == 1 else 32
+
+            def part(ref, k):
+                return ref.at[pl.ds(k * size, size)]
+        else:
+
+            def part(ref, k):
+                return ref.at[k]
+
+        source, target = lax.rem(row + 2, 8), {"row": lax.rem(row + 6, 8)}
+        return part, held, relay_rsem.at[at], relay_ssem.at[at], source, target
+
     def burst(stage, m, half):
         sems = ssem.at[stage * 4 + m * 2 + half], rsem.at[stage * 4 + m * 2 + half]
         if stage == 0:
@@ -270,6 +309,7 @@
                 recv_z.at[m],
                 send_z.at[m, pl.ds(0, 7)],
                 *sems,
+                relay(stage, m, half),
             )
         if stage == 1:
             return Burst(
@@ -280,6 +320,7 @@
                 recv_b.at[m, half],
                 send_b.at[m, pl.ds(0, 7)],
                 *sems,
+                relay(stage, m, half),
             )
         if stage == 2 and half == 1:
             return Burst(
@@ -290,6 +331,7 @@
                 recv_zt.at[m],
                 send_zt.at[m, pl.ds(0, 7)],
                 *sems,
+                relay(stage, m, half),
             )
         if stage == 2:
             return Burst(
@@ -300,6 +342,7 @@
                 recv_bt.at[m],
                 send_bt.at[m, half, pl.ds(0, 7)],
                 *sems,
+                relay(stage, m, half),
             )
         return Burst(
             plane,
@@ -387,13 +430,15 @@
                 ]
             send_zt[m, z] = mix_s[pl.ds(512 + z * 64, 64), :].astype(BF16)
 
-    def triangle(m, gap):
+    def triangle(m, gap, gap_back):
+        burst(1, m, 0).forward()
         burst(0, m, 1).wait()
         to_rows(m, 1)
         burst(1, m, 1).start()
         burst(1, m, 0).wait()
         regroup(m)
         burst(0, m, 0).start()
+        burst(1, m, 1).forward()
         gap()
         burst(0, m, 1).drain()
 
@@ -463,12 +508,15 @@
         for half in range(2):
             burst(1, m, half).drain()
             cross_left(m, half).wait_send()
+        burst(2, m, 0).forward()
+        gap_back()
         burst(3, m, 1).wait()
         regroup_back(m)
         burst(2, m, 1).start()
         burst(2, m, 0).wait()
         to_channels(m, 0)
         burst(3, m, 0).start()
+        burst(2, m, 1).forward()
         burst(2, m, 0).drain()
         burst(3, m, 1).drain()
 
@@ -530,14 +578,14 @@
                 rows = slice(z * 16, z * 16 + 16)
                 gmid_s[2 + m, rows, :] = mix_s[pl.ds(z, 16, stride=8), :]
                 wout_s[2 + m, rows, :] = mix_s[pl.ds(128 + z, 16, stride=8), :].astype(BF16)
-        project((0, 1))
+        project((0,))
 
     edges(0, 0, first_state)
     pl.semaphore_wait(barrier, 30)
     burst(1, 0, 0).start()
     edges(0, 1, first_state)
     burst(0, 0, 1).start()
-    triangle(0, gap_first)
+    triangle(0, gap_first, lambda: project((1,)))
     for half in range(2):
         middle_norm(0, half)
         edges(1, half, second_state)
@@ -557,7 +605,7 @@
             rsem.at[16 + half],
         )
 
-    triangle(1, lambda: project((2, 3)))
+    triangle(1, lambda: project((2,)), lambda: project((3,)))
     for half in range(2):
         middle_norm(1, half)
         for it in range(half * 4, half * 4 + 4):
@@ -799,6 +847,12 @@
             pltpu.SemaphoreType.DMA((3, 16)),
             pltpu.SemaphoreType.DMA((3, 16)),
             pltpu.SemaphoreType.DMA((15,)),
+            pltpu.VMEM((2, 64, 128), BF16),
+            pltpu.VMEM((2, 2, 16, 256), BF16),
+            pltpu.VMEM((2, 16, 256), BF16),
+            pltpu.VMEM((2, 32, 128), BF16),
+            pltpu.SemaphoreType.DMA((8,)),
+            pltpu.SemaphoreType.DMA((8,)),
         ],
         compiler_params=pltpu.CompilerParams(
             collective_id=0, has_side_effects=True, vmem_limit_bytes=60 * 1024 * 1024

time: 95.5 us -> 99.3 us (1.040)
  Pallas kernels: 94.7 us -> 98.6 us
    pallas_call x1, Pallas kernels: 92.7 us -> 96.5 us  [on_device(): pl.pallas_call(block_kernel, out_shape=(jax.ShapeDtypeStruct((1024, 128),...]
where the time goes in v10:
time: 99.3 us; the launch traced here: 99.2 us
  Pallas kernels  98.6 us (99%)
    pallas_call x1, Pallas kernels, on_device(): pl.pallas_call(block_kernel, out_shape=(jax.ShapeDtypeStruct((1024, 128),...  96.5 us
    pallas_call x1, Pallas kernels, on_device(): pl.pallas_call(close_kernel, out_shape=(jax.ShapeDtypeStruct((1024, 128),...  2.05 us

profile of v10, /device:TPU:27, one launch (start us, length us, event | category | flops | bytes accessed | tf_op | source)
XLA Modules:
  0.0 99.2 jit_solution(12157877921885696597)
XLA Ops:
  0.6 96.5 %shard_map.158 = (f32[1024,128]{1,0:T(8,128)}, f32[128,768]{1,0:T(8,128)}) custom-call(bf16[1024,128]{1,0:T(8,128)(2,1)} %bitcast.11, s32[32,32]{1,0:T(8,128)} %refs_1_.1, bf16[2,128,512]{2,1,0:T(8,128)(2,1)} %refs_2_.1, bf16[2,128,128]{2,1,0:T(8,128)(2,1)} %refs_3_.1, bf16[2,128,128]{2,1,0:T(8,128)(2,1)} %refs_4_.1, f32[2,2,128]{2,1,0:T(2,128)} %refs_5_.1, ...), custom_call_target="tpu_custom_call" | custom-call | flops 6000000000 | bytes 15000000 | tf_op jit(solution)/shard_map/pallas_call | solution.py:798
  97.2 2.0 %shard_map.159 = (f32[1024,128]{1,0:T(8,128)}, f32[128,768]{1,0:T(8,128)}) custom-call(f32[1024,128]{1,0:T(8,128)} %get-tuple-element.6.pair_ref, f32[128,768]{1,0:T(8,128)} %get-tuple-element.7.tokens_ref), custom_call_target="tpu_custom_call" | custom-call | tf_op jit(solution)/shard_map/pallas_call | solution.py:864

commit v11 on v9

--- a/solution.py
+++ b/solution.py
@@ -160,6 +160,7 @@
         many_ssem,
         many_rsem,
         load_sem,
+        out_sem,
     ) = refs[32:]
     group, row, col = (lax.axis_index(name) for name in ("group", "row", "col"))
     big = group * 8 + row
@@ -414,8 +415,8 @@
         if m == 0:
             for half in range(2):
                 arrive(half)
+                cross_right(half).start()
                 cross_left(m, half).start()
-                cross_right(half).start()
             right = jnp.concatenate(
                 [
                     recv_b[m, half, s % 4, core, s // 4, 1]
@@ -428,12 +429,12 @@
                 mm(recv_b[m, half, :, :, :, 0].reshape(256, 256), right, NT) for half in range(2)
             ]
             for half in range(2):
-                cross_left(m, half).wait_recv()
                 cross_right(half).wait_recv()
             right = jnp.concatenate(
                 [x_right[half, s % 4, s // 4] for s in range(8) for half in range(2)], axis=0
             )
             for half in range(2):
+                cross_left(m, half).wait_recv()
                 total = own[half] + mm(x_left[m, half].reshape(256, 256), right, NT)
                 send_bt[m, half] = total.astype(BF16).reshape(8, 2, 16, 256)
                 send_back(half)
@@ -545,6 +546,10 @@
     burst(3, 0, 0).drain()
     burst(2, 0, 1).drain()
 
+    def write_pair(half):
+        rows = pl.ds(half * 512, 512)
+        return pltpu.make_async_copy(z_s.at[rows], out_ref.at[rows], out_sem.at[half])
+
     def to_head(half):
         return Burst(
             heads,
@@ -562,11 +567,12 @@
         middle_norm(1, half)
         for it in range(half * 4, half * 4 + 4):
             z = z_s[pl.ds(it * 128, 128), :] + update(1, it)
-            out_ref[pl.ds(it * 128, 128), :] = z
+            z_s[pl.ds(it * 128, 128), :] = z
             zn = normalize(z, held["bgain"][...]).astype(BF16)
             bias = mm(held["bw"][...], zn, NT).astype(BF16).astype(F32)
             heads_s[half, pl.ds(it % 4, 16, stride=8), :] = bias
         to_head(half).start()
+        write_pair(half).start()
 
     def along(half, offset):
         block = bias_s.at[big, pl.ds(half * 16, 16)]
@@ -681,12 +687,14 @@
     first = own + mm(recv_o[...].reshape(768, 128), held["wout"][...], TN)
     xn2 = normalize(first, held["tgain"][...].reshape(1, 768)).astype(BF16)
     total = first
-    for j in range(4):
-        up = mm(xn2, held["wup"][:, j * 384 : (j + 1) * 384])
-        side = mm(xn2, held["wup"][:, 1536 + j * 384 : 1536 + (j + 1) * 384])
+    for j in range(3):
+        up = mm(xn2, held["wup"][:, j * 512 : (j + 1) * 512])
+        side = mm(xn2, held["wup"][:, 1536 + j * 512 : 1536 + (j + 1) * 512])
         hidden = (up * sigmoid(up) * side).astype(BF16)
-        total += mm(hidden, held["wdown"][j * 384 : (j + 1) * 384, :])
+        total += mm(hidden, held["wdown"][j * 512 : (j + 1) * 512, :])
     tok_ref[...] = total
+    for half in range(2):
+        write_pair(half).wait()
 
 
 def close_kernel(pair_ref, tokens_ref, pair_out, tokens_out, pair_s, tokens_s, in_sem, out_sem):
@@ -754,7 +762,7 @@
             jax.ShapeDtypeStruct((128, 768), F32),
         ),
         in_specs=[hbm] * 15,
-        out_specs=(vmem, vmem),
+        out_specs=(hbm, vmem),
         scratch_shapes=[pltpu.VMEM(x.shape, x.dtype) for x in operands]
         + [
             pltpu.VMEM((1024, 128), F32),
@@ -799,6 +807,7 @@
             pltpu.SemaphoreType.DMA((3, 16)),
             pltpu.SemaphoreType.DMA((3, 16)),
             pltpu.SemaphoreType.DMA((15,)),
+            pltpu.SemaphoreType.DMA((2,)),
         ],
         compiler_params=pltpu.CompilerParams(
             collective_id=0, has_side_effects=True, vmem_limit_bytes=60 * 1024 * 1024

time: 95.5 us -> 94.8 us (level)
  no operation moved by 1% of the time
where the time goes in v11:
time: 94.8 us; the launch traced here: 94.7 us
  Pallas kernels  94 us (99%)
    pallas_call x1, Pallas kernels, on_device(): pl.pallas_call(block_kernel, out_shape=(jax.ShapeDtypeStruct((1024, 128),...  92 us
    pallas_call x1, Pallas kernels, on_device(): pl.pallas_call(close_kernel, out_shape=(jax.ShapeDtypeStruct((1024, 128),...  2.05 us

profile of v11, /device:TPU:27, one launch (start us, length us, event | category | flops | bytes accessed | tf_op | source)
XLA Modules:
  0.0 94.7 jit_solution(5214584738793075007)
XLA Ops:
  0.6 92.0 %shard_map.158 = (f32[1024,128]{1,0:T(8,128)}, f32[128,768]{1,0:T(8,128)}) custom-call(bf16[1024,128]{1,0:T(8,128)(2,1)} %bitcast.11, s32[32,32]{1,0:T(8,128)} %refs_1_.1, bf16[2,128,512]{2,1,0:T(8,128)(2,1)} %refs_2_.1, bf16[2,128,128]{2,1,0:T(8,128)(2,1)} %refs_3_.1, bf16[2,128,128]{2,1,0:T(8,128)(2,1)} %refs_4_.1, f32[2,2,128]{2,1,0:T(2,128)} %refs_5_.1, ...), custom_call_target="tpu_custom_call" | custom-call | flops 6000000000 | bytes 15000000 | tf_op jit(solution)/shard_map/pallas_call | solution.py:758
  92.6 2.0 %shard_map.159 = (f32[1024,128]{1,0:T(8,128)}, f32[128,768]{1,0:T(8,128)}) custom-call(f32[1024,128]{1,0:T(8,128)} %get-tuple-element.6.pair_ref, f32[128,768]{1,0:T(8,128)} %get-tuple-element.7.tokens_ref), custom_call_target="tpu_custom_call" | custom-call | tf_op jit(solution)/shard_map/pallas_call | solution.py:819
